TPU v7x, 32 devices: a whole 2x2x4 slice. The times are simulated.
32 devices in a mesh: outer: 8 (over z, core), inner: 4 (over y, x).
Axes of the slice: x: 2, y: 2, z: 4, core: 2. Of those that a mesh axis runs over, the one named last changes fastest.
Arguments:
- queries: bfloat16 [4096, 32, 128], P(('outer', 'inner')), may hold values from -8 to 8
- keys: bfloat16 [4096, 4, 128], P(('outer', 'inner')), may hold values from -8 to 8
- values: bfloat16 [4096, 4, 128], P(('outer', 'inner')), may hold values from -6 to 6
- positions: int32 [4096], P(('outer', 'inner')), may hold values from 0 to 4095, as said below
Outputs:
- attended: bfloat16 [4096, 32, 128], P(('outer', 'inner'))
Inputs may be any that keep to these rules, and one draw needn't show every extreme that they name: positions is a permutation of the numbers 0 to 4095 made of runs of 64 consecutive ascending positions starting at multiples of 64; runs are laid out in an order drawn from the seed.
All inputs are finite; a program needn't handle non-finite values.
Results may differ from a plain program's by a relative error of at most 0.0045.
Values may be sent and summed in bfloat16 or wider, within the bound.
No kernel may reach another device: no remote copies, remote signals or barrier semaphores. Data moves between devices by JAX's collectives and lax.ppermute only.
A program may use at most 128 MiB of HBM per device.

v0:
```python
import jax
import jax.numpy as jnp
from jax import lax
from jax.sharding import PartitionSpec as P


def per_device(queries, keys, values, positions):
    devices_all = lax.axis_size("outer") * lax.axis_size("inner")
    span_len = positions.shape[0] * devices_all // 2
    q_rows, q_pos = (queries, positions)
    tok_rows, heads_q, head_dim = q_rows.shape
    heads_kv = keys.shape[1]
    group = heads_q // heads_kv
    scale = 1.0 / head_dim**0.5
    q_group = q_rows.reshape(tok_rows, heads_kv, group, head_dim)
    q_span = q_pos // span_len

    def update(carry, key_blk, val_blk, mask):
        run_max, run_total, run_acc = carry
        score = (
            jnp.einsum("qgjd,kgd->gjqk", q_group, key_blk, preferred_element_type=jnp.float32)
            * scale
        )
        score = jnp.where(mask[None, None], score, -1e30)
        new_max = jnp.maximum(run_max, jnp.max(score, axis=-1))
        factor = jnp.exp(run_max - new_max)
        weight = jnp.where(mask[None, None], jnp.exp(score - new_max[..., None]), 0.0)
        run_total = run_total * factor + jnp.sum(weight, axis=-1)
        part_sum = jnp.einsum(
            "gjqk,kgd->gjqd",
            weight.astype(jnp.bfloat16),
            val_blk,
            preferred_element_type=jnp.float32,
        )
        run_acc = run_acc * factor[..., None] + part_sum
        return (new_max, run_total, run_acc)

    def one_block(carry, blk):
        key_blk, val_blk, pos_blk = blk
        mask = (pos_blk[None, :] <= q_pos[:, None]) & (
            pos_blk[None, :] // span_len == q_span[:, None]
        )
        live = jnp.any(mask)
        result = lax.cond(
            live, lambda state: update(state, key_blk, val_blk, mask), lambda state: state, carry
        )
        return (result, None)

    init = (
        jnp.full((heads_kv, group, tok_rows), -1e30, jnp.float32),
        jnp.zeros((heads_kv, group, tok_rows), jnp.float32),
        jnp.zeros((heads_kv, group, tok_rows, head_dim), jnp.float32),
    )
    group_k, group_v, group_p = (
        lax.all_gather(keys, "inner", axis=0, tiled=True),
        lax.all_gather(values, "inner", axis=0, tiled=True),
        lax.all_gather(positions, "inner", axis=0, tiled=True),
    )
    carry = init
    key_p = lax.all_gather(group_k, "outer", axis=0, tiled=True)
    val_p = lax.all_gather(group_v, "outer", axis=0, tiled=True)
    pos_p = lax.all_gather(group_p, "outer", axis=0, tiled=True)
    rows = key_p.shape[0]
    step_rows = 1024
    count = rows // step_rows
    stacked = (
        key_p.reshape(count, step_rows, heads_kv, head_dim),
        val_p.reshape(count, step_rows, heads_kv, head_dim),
        pos_p.reshape(count, step_rows),
    )
    carry, unused = lax.scan(one_block, carry, stacked)
    run_max, run_total, run_acc = carry
    mixed = run_acc / run_total[..., None]
    result = (
        jnp.transpose(mixed, (2, 0, 1, 3)).reshape(tok_rows, heads_q, head_dim).astype(jnp.bfloat16)
    )
    return result


def solution(mesh):
    in_specs = (
        P(("outer", "inner"), None, None),
        P(("outer", "inner"), None, None),
        P(("outer", "inner"), None, None),
        P(("outer", "inner")),
    )
    out_specs = P(("outer", "inner"), None, None)
    return jax.shard_map(
        per_device, mesh=mesh, in_specs=in_specs, out_specs=out_specs, check_vma=False
    )
```

profile of v0, /device:TPU:1, one launch (start us, length us, event | category | flops | bytes accessed | tf_op | source)
XLA Modules:
  0.0 193.7 jit_solution(15673281830981213140)
XLA Ops:
  6.5 0.0 copy-start
  6.5 0.0 all-gather.5.cloned.1.call-start
  6.5 0.9 copy.16
  7.5 9.9 %all_gather.20 = bf16[512,4,128]{2,0,1:T(8,128)(2,1)} all-gather(bf16[128,4,128]{2,0,1:T(8,128)(2,1)S(1)} %copy.16), channel_id=1, replica_groups=mesh['outer'=8,'inner'=4] {'inner'}, dimensions={0}, use_global_device_ids=true | all-gather | bytes 655360 | tf_op jit(solution)/shard_map/all_gather | solution.py:55
  17.3 0.0 all-gather.5.cloned.1.call-update
  17.4 0.0 all-gather.7.cloned.1.call-start
  17.4 0.9 copy.18
  18.3 9.0 %all_gather.22 = bf16[512,4,128]{2,0,1:T(8,128)(2,1)} all-gather(bf16[128,4,128]{2,0,1:T(8,128)(2,1)S(1)} %copy.18), channel_id=1, replica_groups=mesh['outer'=8,'inner'=4] {'inner'}, dimensions={0}, use_global_device_ids=true | all-gather | bytes 655360 | tf_op jit(solution)/shard_map/all_gather | solution.py:56
  27.3 0.0 all-gather.7.cloned.1.call-update
  27.3 6.2 %all-gather = s32[4,1,128]{2,1,0:T(1,128)S(1)} all-gather(s32[1,1,128]{2,1,0:T(1,128)} %bitcast.49), channel_id=1, replica_groups=mesh['outer'=8,'inner'=4] {'inner'}, dimensions={0}, use_global_device_ids=true | all-gather | bytes 2560 | tf_op jit(solution)/shard_map/all_gather | solution.py:57
  33.5 18.6 %all-gather.1 = s32[8,1,512]{2,1,0:T(1,128)S(1)} all-gather(s32[1,1,512]{2,1,0:T(1,128)S(1)} %bitcast.50), channel_id=1, replica_groups=mesh['outer'=8,'inner'=4] {'outer'}, dimensions={0}, use_global_device_ids=true | all-gather | bytes 18432 | tf_op jit(solution)/shard_map/all_gather | solution.py:62
  52.2 1.6 copy.17
  53.8 0.7 and_select_fusion.1
  54.5 12.7 %all-gather.5.cloned.1.call-done = bf16[4096,4,128]{2,0,1:T(8,128)(2,1)} async-done(((bf16[512,4,128]{2,0,1:T(8,128)(2,1)}), bf16[4096,4,128]{2,0,1:T(8,128)(2,1)}) %all-gather.5.cloned.1.call-update) | async-done | bytes 4194320 | tf_op jit(solution)/shard_map/all_gather | solution.py:60
  67.2 4.5 %copy.19 = bf16[4,1024,4,128]{3,1,2,0:T(8,128)(2,1)} copy(bf16[4,1024,4,128]{3,1,0,2:T(8,128)(2,1)} %bitcast.45) | data formatting | bytes 8388608 | tf_op jit(solution)/shard_map/while | solution.py:71
  71.8 42.9 %all-gather.7.cloned.1.call-done = bf16[4096,4,128]{2,0,1:T(8,128)(2,1)} async-done(((bf16[512,4,128]{2,0,1:T(8,128)(2,1)}), bf16[4096,4,128]{2,0,1:T(8,128)(2,1)}) %all-gather.7.cloned.1.call-update) | async-done | bytes 4194320 | tf_op jit(solution)/shard_map/all_gather | solution.py:61
  114.7 4.6 %copy.20 = bf16[4,1024,4,128]{3,1,2,0:T(8,128)(2,1)} copy(bf16[4,1024,4,128]{3,1,0,2:T(8,128)(2,1)} %bitcast.46) | data formatting | bytes 8388608 | tf_op jit(solution)/shard_map/while | solution.py:71
  119.2 0.2 broadcast_in_dim.44
  119.5 0.0 copy-done
  119.5 65.0 %while.16 = (s32[]{:T(128)}, f32[4,8,128]{2,1,0:T(8,128)S(1)}, f32[4,8,128]{2,1,0:T(8,128)S(1)}, f32[4,8,128,128]{3,2,1,0:T(8,128)S(1)}, s32[4,1024]{1,0:T(4,128...) while((s32[]{:T(128)}, f32[4,8,128]{2,1,0:T(8,128)S(1)}, ...), condition=%wide.region_6.7_spmd, body=%wide.region_0.6_spmd.sunk | while | flops 2203606016 | bytes 58480880 | solution.py:71
  119.5 0.9 fusion.22
  121.0 14.7 %conditional.2 = ((f32[4,8,128]{2,1,0:T(8,128)S(1)}, f32[4,8,128]{2,1,0:T(8,128)S(1)}, f32[4,8,128,128]{3,2,1,0:T(8,128)S(1)})) conditional(s32[]{:T(128)} %convert_element_type.31, (f32[4,8,128]{2,1,0:T(8,128)S(1)}, f32[4,8,128]{2,1,0:T(8,128)S(1)}, f32[4,8,128,128]{3,2,1,0:T(8,128)S(1)}) %tuple.51, (pred[128,1024]{0,1:T(8,128)(4,1)S(1)}, ...), branch_computations={%region_2.2_spmd, %region_3.5_spmd} | conditional | flops 2203066368 | bytes 58328096 | solution.py:44
  121.0 3.7 %fusion = (f32[4,8,128]{2,1,0:T(8,128)S(1)}, f32[4,1024,128,8]{2,1,3,0:T(8,128)S(1)}) fusion(pred[128,1024]{0,1:T(8,128)(4,1)S(1)} %get-tuple-element.191, bf16[128,4,8,128]{3,0,2,1:T(8,128)(2,1)S(1)} %get-tuple-element.194, bf16[4,1024,4,128]{3,1,2,0:T(8,128)(2,1)} %get-tuple-element.192, s32[]{:T(128)} %get-tuple-element.193), kind=kOutput, calls=%fused_computation.2 | convolution fusion | flops 1086320640 | bytes 19022336 | tf_op jit(solution)/shard_map/while/body/eval_jaxpr/cond/branch_1_fun/qgjd,kgd->gjqk/dot_general | solution.py:21
  124.7 4.2 %fusion.2 = f32[4,8,128]{2,1,0:T(8,128)S(1)} fusion(f32[4,1024,128,8]{2,1,3,0:T(8,128)S(1)} %get-tuple-element.263, f32[4,8,128]{2,1,0:T(8,128)S(1)} %max.4, pred[128,1024]{0,1:T(8,128)(4,1)S(1)} %get-tuple-element.191), kind=kLoop, calls=%fused_computation.4 | loop fusion | flops 20967424 | bytes 16941056 | tf_op jit(solution)/shard_map/while/body/eval_jaxpr/cond/branch_1_fun/reduce_sum | solution.py:28
  129.0 6.7 %multiply_add_fusion = f32[4,8,128,128]{3,2,1,0:T(8,128)S(1)} fusion(f32[4,8,128,128]{3,2,1,0:T(8,128)S(1)} %get-tuple-element.196, f32[4,1024,128,8]{2,1,3,0:T(8,128)S(1)} %get-tuple-element.263, f32[4,8,128]{2,1,0:T(8,128)S(1)} %max.4, pred[128,1024]{0,1:T(8,128)(4,1)S(1)} %get-tuple-element.191, bf16[4,1024,4,128]{3,1,2,0:T(8,128)(2,1)} %get-tuple-element.197, ...), kind=kOutput, calls=%fused_computation.7 | convolution fusion | flops 1095761920 | bytes 22184448 | tf_op jit(solution)/shard_map/while/body/eval_jaxpr/cond/branch_1_fun/gjqk,kgd->gjqd/dot_general | solution.py:29
  135.8 0.9 fusion.22
  137.3 14.7 %conditional.2 = ((f32[4,8,128]{2,1,0:T(8,128)S(1)}, f32[4,8,128]{2,1,0:T(8,128)S(1)}, f32[4,8,128,128]{3,2,1,0:T(8,128)S(1)})) conditional(s32[]{:T(128)} %convert_element_type.31, (f32[4,8,128]{2,1,0:T(8,128)S(1)}, f32[4,8,128]{2,1,0:T(8,128)S(1)}, f32[4,8,128,128]{3,2,1,0:T(8,128)S(1)}) %tuple.51, (pred[128,1024]{0,1:T(8,128)(4,1)S(1)}, ...), branch_computations={%region_2.2_spmd, %region_3.5_spmd} | conditional | flops 2203066368 | bytes 58328096 | solution.py:44
  137.3 3.7 %fusion = (f32[4,8,128]{2,1,0:T(8,128)S(1)}, f32[4,1024,128,8]{2,1,3,0:T(8,128)S(1)}) fusion(pred[128,1024]{0,1:T(8,128)(4,1)S(1)} %get-tuple-element.191, bf16[128,4,8,128]{3,0,2,1:T(8,128)(2,1)S(1)} %get-tuple-element.194, bf16[4,1024,4,128]{3,1,2,0:T(8,128)(2,1)} %get-tuple-element.192, s32[]{:T(128)} %get-tuple-element.193), kind=kOutput, calls=%fused_computation.2 | convolution fusion | flops 1086320640 | bytes 19022336 | tf_op jit(solution)/shard_map/while/body/eval_jaxpr/cond/branch_1_fun/qgjd,kgd->gjqk/dot_general | solution.py:21
  141.0 4.2 %fusion.2 = f32[4,8,128]{2,1,0:T(8,128)S(1)} fusion(f32[4,1024,128,8]{2,1,3,0:T(8,128)S(1)} %get-tuple-element.263, f32[4,8,128]{2,1,0:T(8,128)S(1)} %max.4, pred[128,1024]{0,1:T(8,128)(4,1)S(1)} %get-tuple-element.191), kind=kLoop, calls=%fused_computation.4 | loop fusion | flops 20967424 | bytes 16941056 | tf_op jit(solution)/shard_map/while/body/eval_jaxpr/cond/branch_1_fun/reduce_sum | solution.py:28
  145.2 6.7 %multiply_add_fusion = f32[4,8,128,128]{3,2,1,0:T(8,128)S(1)} fusion(f32[4,8,128,128]{3,2,1,0:T(8,128)S(1)} %get-tuple-element.196, f32[4,1024,128,8]{2,1,3,0:T(8,128)S(1)} %get-tuple-element.263, f32[4,8,128]{2,1,0:T(8,128)S(1)} %max.4, pred[128,1024]{0,1:T(8,128)(4,1)S(1)} %get-tuple-element.191, bf16[4,1024,4,128]{3,1,2,0:T(8,128)(2,1)} %get-tuple-element.197, ...), kind=kOutput, calls=%fused_computation.7 | convolution fusion | flops 1095761920 | bytes 22184448 | tf_op jit(solution)/shard_map/while/body/eval_jaxpr/cond/branch_1_fun/gjqk,kgd->gjqd/dot_general | solution.py:29
  152.0 0.9 fusion.22
  153.5 14.7 %conditional.2 = ((f32[4,8,128]{2,1,0:T(8,128)S(1)}, f32[4,8,128]{2,1,0:T(8,128)S(1)}, f32[4,8,128,128]{3,2,1,0:T(8,128)S(1)})) conditional(s32[]{:T(128)} %convert_element_type.31, (f32[4,8,128]{2,1,0:T(8,128)S(1)}, f32[4,8,128]{2,1,0:T(8,128)S(1)}, f32[4,8,128,128]{3,2,1,0:T(8,128)S(1)}) %tuple.51, (pred[128,1024]{0,1:T(8,128)(4,1)S(1)}, ...), branch_computations={%region_2.2_spmd, %region_3.5_spmd} | conditional | flops 2203066368 | bytes 58328096 | solution.py:44
  153.5 3.7 %fusion = (f32[4,8,128]{2,1,0:T(8,128)S(1)}, f32[4,1024,128,8]{2,1,3,0:T(8,128)S(1)}) fusion(pred[128,1024]{0,1:T(8,128)(4,1)S(1)} %get-tuple-element.191, bf16[128,4,8,128]{3,0,2,1:T(8,128)(2,1)S(1)} %get-tuple-element.194, bf16[4,1024,4,128]{3,1,2,0:T(8,128)(2,1)} %get-tuple-element.192, s32[]{:T(128)} %get-tuple-element.193), kind=kOutput, calls=%fused_computation.2 | convolution fusion | flops 1086320640 | bytes 19022336 | tf_op jit(solution)/shard_map/while/body/eval_jaxpr/cond/branch_1_fun/qgjd,kgd->gjqk/dot_general | solution.py:21
  157.2 4.2 %fusion.2 = f32[4,8,128]{2,1,0:T(8,128)S(1)} fusion(f32[4,1024,128,8]{2,1,3,0:T(8,128)S(1)} %get-tuple-element.263, f32[4,8,128]{2,1,0:T(8,128)S(1)} %max.4, pred[128,1024]{0,1:T(8,128)(4,1)S(1)} %get-tuple-element.191), kind=kLoop, calls=%fused_computation.4 | loop fusion | flops 20967424 | bytes 16941056 | tf_op jit(solution)/shard_map/while/body/eval_jaxpr/cond/branch_1_fun/reduce_sum | solution.py:28
  161.4 6.7 %multiply_add_fusion = f32[4,8,128,128]{3,2,1,0:T(8,128)S(1)} fusion(f32[4,8,128,128]{3,2,1,0:T(8,128)S(1)} %get-tuple-element.196, f32[4,1024,128,8]{2,1,3,0:T(8,128)S(1)} %get-tuple-element.263, f32[4,8,128]{2,1,0:T(8,128)S(1)} %max.4, pred[128,1024]{0,1:T(8,128)(4,1)S(1)} %get-tuple-element.191, bf16[4,1024,4,128]{3,1,2,0:T(8,128)(2,1)} %get-tuple-element.197, ...), kind=kOutput, calls=%fused_computation.7 | convolution fusion | flops 1095761920 | bytes 22184448 | tf_op jit(solution)/shard_map/while/body/eval_jaxpr/cond/branch_1_fun/gjqk,kgd->gjqd/dot_general | solution.py:29
  168.3 0.9 fusion.22
  169.7 14.7 %conditional.2 = ((f32[4,8,128]{2,1,0:T(8,128)S(1)}, f32[4,8,128]{2,1,0:T(8,128)S(1)}, f32[4,8,128,128]{3,2,1,0:T(8,128)S(1)})) conditional(s32[]{:T(128)} %convert_element_type.31, (f32[4,8,128]{2,1,0:T(8,128)S(1)}, f32[4,8,128]{2,1,0:T(8,128)S(1)}, f32[4,8,128,128]{3,2,1,0:T(8,128)S(1)}) %tuple.51, (pred[128,1024]{0,1:T(8,128)(4,1)S(1)}, ...), branch_computations={%region_2.2_spmd, %region_3.5_spmd} | conditional | flops 2203066368 | bytes 58328096 | solution.py:44
  169.8 3.7 %fusion = (f32[4,8,128]{2,1,0:T(8,128)S(1)}, f32[4,1024,128,8]{2,1,3,0:T(8,128)S(1)}) fusion(pred[128,1024]{0,1:T(8,128)(4,1)S(1)} %get-tuple-element.191, bf16[128,4,8,128]{3,0,2,1:T(8,128)(2,1)S(1)} %get-tuple-element.194, bf16[4,1024,4,128]{3,1,2,0:T(8,128)(2,1)} %get-tuple-element.192, s32[]{:T(128)} %get-tuple-element.193), kind=kOutput, calls=%fused_computation.2 | convolution fusion | flops 1086320640 | bytes 19022336 | tf_op jit(solution)/shard_map/while/body/eval_jaxpr/cond/branch_1_fun/qgjd,kgd->gjqk/dot_general | solution.py:21
  173.4 4.2 %fusion.2 = f32[4,8,128]{2,1,0:T(8,128)S(1)} fusion(f32[4,1024,128,8]{2,1,3,0:T(8,128)S(1)} %get-tuple-element.263, f32[4,8,128]{2,1,0:T(8,128)S(1)} %max.4, pred[128,1024]{0,1:T(8,128)(4,1)S(1)} %get-tuple-element.191), kind=kLoop, calls=%fused_computation.4 | loop fusion | flops 20967424 | bytes 16941056 | tf_op jit(solution)/shard_map/while/body/eval_jaxpr/cond/branch_1_fun/reduce_sum | solution.py:28
  177.7 6.7 %multiply_add_fusion = f32[4,8,128,128]{3,2,1,0:T(8,128)S(1)} fusion(f32[4,8,128,128]{3,2,1,0:T(8,128)S(1)} %get-tuple-element.196, f32[4,1024,128,8]{2,1,3,0:T(8,128)S(1)} %get-tuple-element.263, f32[4,8,128]{2,1,0:T(8,128)S(1)} %max.4, pred[128,1024]{0,1:T(8,128)(4,1)S(1)} %get-tuple-element.191, bf16[4,1024,4,128]{3,1,2,0:T(8,128)(2,1)} %get-tuple-element.197, ...), kind=kOutput, calls=%fused_computation.7 | convolution fusion | flops 1095761920 | bytes 22184448 | tf_op jit(solution)/shard_map/while/body/eval_jaxpr/cond/branch_1_fun/gjqk,kgd->gjqd/dot_general | solution.py:29
  184.4 0.7 fusion.18
  185.2 1.6 copy.26
  (20 shorter events, 0.3 us)
Async XLA Ops:
  6.5 112.9 %copy-start = (s32[128]{0:T(128)S(1)}, s32[128]{0:T(128)}, u32[]{:S(2)}) copy-start(s32[128]{0:T(128)} %param.11) | copy-start | bytes 1540
  6.5 60.7 %all-gather.5.cloned.1.call-start = ((), (), s32[]{:S(2)}) async-start(), calls=%async_computation | async-start | bytes 4718592 | tf_op jit(solution)/shard_map/all_gather | solution.py:60
  17.4 97.3 %all-gather.7.cloned.1.call-start = ((), (), s32[]{:S(2)}) async-start(), calls=%async_computation.1 | async-start | bytes 4718592 | tf_op jit(solution)/shard_map/all_gather | solution.py:61
Sparse Core Ops, SparseCore 0:
  17.5 49.6 all-gather.4
  68.8 45.7 all-gather.6
where the time goes:
time: 194 us
  waiting for transfers between devices  55.7 us (29%)
  blocking collectives  43.6 us (22%)
  matrix products  41.6 us (21%)
  other arithmetic  22.3 us (11%)
  local copies, waits for them, and re-layouts  14.5 us (7%)
  between operations  13.5 us (7%)
  loops' own time  2.57 us (1%)
    all_gather x1, waiting for transfers between devices, per_device(): val_p = lax.all_gather(group_v, 'outer', axis=0, tiled=True)  42.9 us
    dot_general x4, matrix products, update(): jnp.einsum('gjqk,kgd->gjqd', weight.astype(jnp.bfloat16), val_blk, prefer...  26.9 us
    all_gather x1, blocking collectives, per_device(): pos_p = lax.all_gather(group_p, 'outer', axis=0, tiled=True)  18.6 us
    reduce_sum x4, other arithmetic, update(): run_total = run_total * factor + jnp.sum(weight, axis=-1)  16.9 us
    dot_general x4, matrix products, update(): jnp.einsum('qgjd,kgd->gjqk', q_group, key_blk, preferred_element_type=jnp...  14.6 us
    all_gather x1, waiting for transfers between devices, per_device(): key_p = lax.all_gather(group_k, 'outer', axis=0, tiled=True)  12.7 us
    all_gather x1, blocking collectives, per_device(): lax.all_gather(keys, 'inner', axis=0, tiled=True)  9.86 us
    while x2, local copies, waits for them, and re-layouts, per_device(): carry, unused = lax.scan(one_block, carry, stacked)  9.09 us
  transfers between devices with their start and end apart: 2, of which 2 were waited for; matrix products, arithmetic and copies ran while one was open for 4% of the time, Pallas kernels for 0%

commit v1 on v0

v1 whole, which is shorter than its diff:
```python
import functools
import math

import jax
import jax.numpy as jnp
from jax import lax
from jax.experimental import pallas as pl
from jax.experimental.pallas import tpu as pltpu
from jax.sharding import PartitionSpec as P

RUN = 64
TILE = 4
AXES = ("outer", "inner")


def flash(q, k, v, state, mask, factor):
    top, total, mixed = state
    score = lax.dot_general(
        q, k, (((1,), (1,)), ((), ())), preferred_element_type=jnp.float32
    )
    score = mask(score)
    parts = [score[:, c : c + 128] for c in range(0, score.shape[1], 128)]
    new = functools.reduce(jnp.maximum, parts)
    new = jnp.max(new, axis=1, keepdims=True)
    if top is None:
        new = jnp.broadcast_to(new, parts[0].shape)
    else:
        new = jnp.maximum(top, new)
    weights = [jnp.exp2((part - new) * factor) for part in parts]
    part_total = functools.reduce(jnp.add, weights)
    part_mixed = lax.dot_general(
        jnp.concatenate([w.astype(jnp.bfloat16) for w in weights], axis=1),
        v,
        (((1,), (0,)), ((), ())),
        preferred_element_type=jnp.float32,
    )
    if top is None:
        return new, part_total, part_mixed
    decay = jnp.exp2((top - new) * factor)
    return new, total * decay + part_total, mixed * decay + part_mixed


def attend_kernel(group, factor, half, first, last, blocks, own_ids, q_ref, *refs):
    heads_kv = q_ref.shape[1]
    rows = q_ref.shape[2]
    run_rows = 2 * heads_kv * RUN
    kv_refs, refs = refs[:blocks], refs[blocks:]
    if first:
        own_ref, refs = refs[0], refs[1:]
    else:
        refs = refs[3:]
    if last:
        out_ref, refs = refs[0], refs[1:]
    top_ref, total_ref, mixed_ref, buf = refs

    if first:
        row_at = lax.broadcasted_iota(jnp.int32, (rows, 2 * RUN), 0) // group
        col_at = lax.broadcasted_iota(jnp.int32, (rows, 2 * RUN), 1)
        for a in range(2):
            mine, other = own_ids[a], own_ids[1 - a]
            seen = (other < mine) & ((other >= half) == (mine >= half))
            reach = jnp.where(seen, RUN, 0)
            if a == 0:
                live = (col_at <= row_at) | ((col_at >= RUN) & (col_at < RUN + reach))
            else:
                live = (col_at < reach) | ((col_at >= RUN) & (col_at - RUN <= row_at))
            for h in range(heads_kv):
                k, v = (
                    jnp.concatenate(
                        [
                            own_ref[r * run_rows + g * RUN : r * run_rows + (g + 1) * RUN]
                            for r in range(2)
                        ]
                    )
                    for g in (h, heads_kv + h)
                )
                top_ref[a, h], total_ref[a, h], mixed_ref[a, h] = flash(
                    q_ref[a, h],
                    k,
                    v,
                    (None, None, None),
                    lambda score: jnp.where(live, score, -jnp.inf),
                    factor,
                )

    flags = [[], []]
    for start in range(0, blocks, 8):
        some = kv_refs[start : start + 8]
        ids = jnp.concatenate([ref[2 * run_rows :] for ref in some]).astype(jnp.float32)
        row = lax.broadcasted_iota(jnp.int32, ids.shape, 0)
        lane = lax.broadcasted_iota(jnp.int32, ids.shape, 1)
        bit = jnp.left_shift(1, 2 * (row // 16) + lane // RUN)
        bit = jnp.where((row % 16 == 0) & (lane % RUN == 0), bit, 0).astype(jnp.float32)
        for a in range(2):
            mine = own_ids[a].astype(jnp.float32)
            low = jnp.where(mine >= half, float(half), 0.0)
            seen = (ids < mine) & (ids >= low)
            bits = jnp.sum(jnp.where(seen, bit, 0.0)).astype(jnp.int32)
            flags[a] += [(bits >> n) & 1 for n in range(2 * len(some))]

    col = lax.broadcasted_iota(jnp.int32, (8, TILE * RUN), 1)
    for a in range(2):
        count = jnp.int32(0)
        for n in range(2 * blocks):

            @pl.when(flags[a][n] == 1)
            def _():
                at = (n % 2) * run_rows
                buf[a, count] = kv_refs[n // 2][at : at + run_rows]

            count = count + flags[a][n]
        for s in range(TILE - 1):
            buf[a, count + s] = jnp.zeros(buf.shape[2:], buf.dtype)

        def step(item, carry):
            bias = jnp.where(col < (count - item * TILE) * RUN, 0.0, -jnp.inf)[:1]
            runs = pl.ds(item * TILE, TILE)
            for h in range(heads_kv):
                k = buf[a, runs, h * RUN : (h + 1) * RUN, :]
                v = buf[a, runs, (heads_kv + h) * RUN : (heads_kv + h + 1) * RUN, :]
                top_ref[a, h], total_ref[a, h], mixed_ref[a, h] = flash(
                    q_ref[a, h],
                    k.reshape(TILE * RUN, -1),
                    v.reshape(TILE * RUN, -1),
                    (top_ref[a, h], total_ref[a, h], mixed_ref[a, h]),
                    lambda score: score + bias,
                    factor,
                )
            return carry

        lax.fori_loop(0, (count + TILE - 1) // TILE, step, 0)

    if last:
        for a in range(2):
            for h in range(0, heads_kv, 2):
                done = []
                for g in (h, h + 1):
                    total = jnp.sum(total_ref[a, g], axis=1, keepdims=True)
                    done.append((mixed_ref[a, g] / total).reshape(RUN, group, -1))
                out_ref[a * RUN : (a + 1) * RUN, h * group : (h + 2) * group, :] = (
                    jnp.concatenate(done, axis=1).astype(out_ref.dtype)
                )


def attend(own_ids, q, kvs, own, state, out, group, half, factor):
    first, last, blocks = own is not None, out is not None, len(kvs)
    operands = [q, *kvs] + ([own] if first else list(state))
    lanes = jax.ShapeDtypeStruct(q.shape[:3] + (128,), jnp.float32)
    carried = [lanes, lanes, jax.ShapeDtypeStruct(q.shape, jnp.float32)]
    vmem = pl.BlockSpec(memory_space=pltpu.VMEM)
    shapes = ([out] if last else []) + carried
    aliases = {}
    if not first:
        aliases = {2 + blocks + n: int(last) + n for n in range(3)}
    run_rows = 2 * q.shape[1] * RUN
    results = pl.pallas_call(
        functools.partial(attend_kernel, group, factor, half, first, last, blocks),
        out_shape=shapes,
        grid_spec=pltpu.PrefetchScalarGridSpec(
            num_scalar_prefetch=1,
            grid=(),
            in_specs=[vmem] * len(operands),
            out_specs=[vmem] * len(shapes),
            scratch_shapes=[
                pltpu.VMEM((2, 2 * blocks + TILE - 1, run_rows, q.shape[3]), q.dtype)
            ],
        ),
        input_output_aliases=aliases,
        compiler_params=pltpu.CompilerParams(vmem_limit_bytes=24 * 1024 * 1024),
        cost_estimate=pl.CostEstimate(
            flops=blocks * RUN * q.size * 4, bytes_accessed=q.size * 16, transcendentals=0
        ),
        name="attend",
    )(own_ids, *operands)
    return results[0] if last else results


def per_device(queries, keys, values, positions):
    outer, inner = lax.axis_size("outer"), lax.axis_size("inner")
    tokens, heads_q, head_dim = queries.shape
    heads_kv = keys.shape[1]
    group = heads_q // heads_kv
    half = tokens // RUN * outer * inner // 2
    factor = math.log2(math.e) / math.sqrt(head_dim)

    chips = outer // 2
    ring = list(range(inner // 2)) + list(range(inner - 1, inner // 2 - 1, -1))
    after = {ring[n]: ring[(n + 1) % inner] for n in range(inner)}
    before = {there: here for here, there in after.items()}

    def permute(x, to):
        pairs = []
        for z in range(chips):
            for core in range(2):
                for place in range(inner):
                    nz, ncore, nplace = to(z, core, place)
                    pairs.append(
                        (
                            (2 * z + core) * inner + place,
                            (2 * nz + ncore) * inner + nplace,
                        )
                    )
        return lax.ppermute(x, AXES, pairs)

    def along_z(x, step):
        return permute(x, lambda z, core, place: ((z + step) % chips, core, place))

    def around(x):
        return permute(
            x, lambda z, core, place: (z, core, (before if core else after)[place])
        )

    def other_core(x):
        return permute(x, lambda z, core, place: (z, 1 - core, place))

    kv = jnp.concatenate(
        [x.reshape(2, RUN, heads_kv, head_dim) for x in (keys, values)], axis=2
    ).transpose(0, 2, 1, 3)
    numbers = (positions // RUN).astype(jnp.bfloat16)
    own = jnp.concatenate(
        [
            kv.reshape(-1, head_dim),
            jnp.broadcast_to(numbers[None, :], (16, head_dim)),
        ]
    )
    own_ids = (positions[::RUN] // RUN).astype(jnp.int32)
    q = (
        queries.reshape(2, RUN, heads_kv, group, head_dim)
        .transpose(0, 2, 1, 3, 4)
        .reshape(2, heads_kv, RUN * group, head_dim)
    )

    starts = [own] + [along_z(own, step) for step in range(1, chips)]
    state = None
    for n, start in enumerate(starts):
        mine = [start]
        for _ in range(inner - 1):
            mine.append(around(mine[-1]))
        theirs = [other_core(x) for x in mine]
        kvs = mine[1:] + theirs if n == 0 else mine + theirs
        last = n == chips - 1
        state = attend(
            own_ids,
            q,
            kvs,
            own if n == 0 else None,
            state,
            jax.ShapeDtypeStruct(queries.shape, queries.dtype) if last else None,
            group,
            half,
            factor,
        )
    return state


def solution(mesh):
    in_specs = (
        P(("outer", "inner"), None, None),
        P(("outer", "inner"), None, None),
        P(("outer", "inner"), None, None),
        P(("outer", "inner")),
    )
    out_specs = P(("outer", "inner"), None, None)
    return jax.shard_map(
        per_device, mesh=mesh, in_specs=in_specs, out_specs=out_specs, check_vma=False
    )
```

time: 194 us -> 89.5 us (0.46)
  the two profiles are of different devices: /device:TPU:1 before, /device:TPU:29 now
where the time goes in v1:
time: 89.5 us; the launch traced here: 89.7 us
  Pallas kernels  29.6 us (33%)
  starting transfers between devices  26.5 us (30%)
  waiting for transfers between devices  22.1 us (25%)
  local copies, waits for them, and re-layouts  10.6 us (12%)
    pallas_call x4, Pallas kernels, attend(): pl.pallas_call(functools.partial(attend_kernel, group, factor, half, firs...  29.6 us
    ppermute x31, starting transfers between devices, permute(): return lax.ppermute(x, AXES, pairs)  26.5 us
    ppermute x31, waiting for transfers between devices, permute(): return lax.ppermute(x, AXES, pairs)  22.1 us
    unnamed x32, local copies, waits for them, and re-layouts  6.6 us
    reshape x2, local copies, waits for them, and re-layouts, per_device(): x.reshape(2, RUN, heads_kv, head_dim)  1.85 us
  transfers between devices with their start and end apart: 31, of which 10 were waited for; matrix products, arithmetic and copies ran while one was open for 2% of the time, Pallas kernels for 24%

profile of v1, /device:TPU:29, one launch (start us, length us, event | category | flops | bytes accessed | tf_op | source)
XLA Modules:
  0.0 89.7 jit_solution(6359484704043012712)
XLA Ops:
  0.0 0.9 %copy.15 = bf16[2,64,4,128]{3,1,2,0:T(8,128)(2,1)S(1)} copy(bf16[2,64,4,128]{3,2,1,0:T(4,128)(2,1)} %bitcast.17) | data formatting | bytes 262144 | tf_op jit(solution)/shard_map/reshape | solution.py:217
  0.9 0.9 %copy.16 = bf16[2,64,4,128]{3,1,2,0:T(8,128)(2,1)S(1)} copy(bf16[2,64,4,128]{3,2,1,0:T(4,128)(2,1)} %bitcast.18) | data formatting | bytes 262144 | tf_op jit(solution)/shard_map/reshape | solution.py:217
  1.9 0.7 fusion
  2.6 1.3 %collective-permute-start.24 = (bf16[1040,128]{1,0:T(8,128)(2,1)S(1)}, bf16[1040,128]{1,0:T(8,128)(2,1)S(1)}, u32[]{:S(2)}, u32[]{:S(2)}) collective-permute-start(bf16[1040,128]{1,0:T(8,128)(2,1)S(1)} %pad_maximum_fusion.refs_7_), channel_id=1, source_target_pairs={{0,1},{1,3},{2,0},{3,2},{4,6},{5,4},{6,7},{7,5},{8,9},{9,11},{10,8... | collective-permute-start | bytes 798728 | tf_op jit(solution)/shard_map/ppermute | solution.py:203
  3.9 1.3 %collective-permute-start.8 = (bf16[1040,128]{1,0:T(8,128)(2,1)S(1)}, bf16[1040,128]{1,0:T(8,128)(2,1)S(1)}, u32[]{:S(2)}, u32[]{:S(2)}) collective-permute-start(bf16[1040,128]{1,0:T(8,128)(2,1)S(1)} %pad_maximum_fusion.refs_7_), channel_id=1, source_target_pairs={{0,16},{1,17},{2,18},{3,19},{4,20},{5,21},{6,22},{7,23},{8,24},{9,... | collective-permute-start | bytes 798728 | tf_op jit(solution)/shard_map/ppermute | solution.py:203
  5.4 0.7 copy-done
  6.1 2.1 %collective-permute-done.24.refs_0_ = bf16[1040,128]{1,0:T(8,128)(2,1)S(1)} collective-permute-done((bf16[1040,128]{1,0:T(8,128)(2,1)S(1)}, bf16[1040,128]{1,0:T(8,128)(2,1)S(1)}, u32[]{:S(2)}, u32[]{:S(2)}) %collective-permute-start.24) | collective-permute-done | bytes 266272 | tf_op jit(solution)/shard_map/ppermute | solution.py:203
  8.2 1.2 %collective-permute-start.25 = (bf16[1040,128]{1,0:T(8,128)(2,1)S(1)}, bf16[1040,128]{1,0:T(8,128)(2,1)S(1)}, u32[]{:S(2)}, u32[]{:S(2)}) collective-permute-start(bf16[1040,128]{1,0:T(8,128)(2,1)S(1)} %collective-permute-done.24.refs_0_), channel_id=1, source_target_pairs={{0,1},{1,3},{2,0},{3,2},{4,6},{5,4},{6,7},{7,5},{8,9},{9,11},{10,8... | collective-permute-start | bytes 798728 | tf_op jit(solution)/shard_map/ppermute | solution.py:203
  9.4 0.7 copy-done.4
  10.1 0.8 collective-permute-start.28
  11.0 0.7 copy-done.2
  11.7 1.4 %collective-permute-start.17 = (bf16[1040,128]{1,0:T(8,128)(2,1)S(1)}, bf16[1040,128]{1,0:T(8,128)(2,1)S(1)}, u32[]{:S(2)}, u32[]{:S(2)}) collective-permute-start(bf16[1040,128]{1,0:T(8,128)(2,1)S(1)} %collective-permute-done.16.refs_0_), channel_id=1, source_target_pairs={{0,1},{1,3},{2,0},{3,2},{4,6},{5,4},{6,7},{7,5},{8,9},{9,11},{10,8... | collective-permute-start | bytes 798728 | tf_op jit(solution)/shard_map/ppermute | solution.py:203
  13.1 15.2 %collective-permute-done.8.refs_0_ = bf16[1040,128]{1,0:T(8,128)(2,1)S(1)} collective-permute-done((bf16[1040,128]{1,0:T(8,128)(2,1)S(1)}, bf16[1040,128]{1,0:T(8,128)(2,1)S(1)}, u32[]{:S(2)}, u32[]{:S(2)}) %collective-permute-start.8) | collective-permute-done | bytes 266272 | tf_op jit(solution)/shard_map/ppermute | solution.py:203
  28.3 1.4 %collective-permute-start.20 = (bf16[1040,128]{1,0:T(8,128)(2,1)S(1)}, bf16[1040,128]{1,0:T(8,128)(2,1)S(1)}, u32[]{:S(2)}, u32[]{:S(2)}) collective-permute-start(bf16[1040,128]{1,0:T(8,128)(2,1)S(1)} %collective-permute-done.16.refs_0_), channel_id=1, source_target_pairs={{0,4},{1,5},{2,6},{3,7},{4,0},{5,1},{6,2},{7,3},{8,12},{9,13},{10,... | collective-permute-start | bytes 798728 | tf_op jit(solution)/shard_map/ppermute | solution.py:203
  29.7 1.2 %collective-permute-start.9 = (bf16[1040,128]{1,0:T(8,128)(2,1)S(1)}, bf16[1040,128]{1,0:T(8,128)(2,1)S(1)}, u32[]{:S(2)}, u32[]{:S(2)}) collective-permute-start(bf16[1040,128]{1,0:T(8,128)(2,1)S(1)} %collective-permute-done.8.refs_0_), channel_id=1, source_target_pairs={{0,1},{1,3},{2,0},{3,2},{4,6},{5,4},{6,7},{7,5},{8,9},{9,11},{10,8... | collective-permute-start | bytes 798728 | tf_op jit(solution)/shard_map/ppermute | solution.py:203
  31.1 0.7 copy-done.8
  31.9 1.0 %collective-permute-start.1 = (bf16[1040,128]{1,0:T(8,128)(2,1)S(1)}, bf16[1040,128]{1,0:T(8,128)(2,1)S(1)}, u32[]{:S(2)}, u32[]{:S(2)}) collective-permute-start(bf16[1040,128]{1,0:T(8,128)(2,1)S(1)} %collective-permute-done.refs_0_), channel_id=1, source_target_pairs={{0,1},{1,3},{2,0},{3,2},{4,6},{5,4},{6,7},{7,5},{8,9},{9,11},{10,8... | collective-permute-start | bytes 798728 | tf_op jit(solution)/shard_map/ppermute | solution.py:203
  32.8 0.5 collective-permute-start.26
  33.4 0.8 collective-permute-start.29
  34.1 0.7 copy-done.6
  35.2 1.2 %collective-permute-start.18 = (bf16[1040,128]{1,0:T(8,128)(2,1)S(1)}, bf16[1040,128]{1,0:T(8,128)(2,1)S(1)}, u32[]{:S(2)}, u32[]{:S(2)}) collective-permute-start(bf16[1040,128]{1,0:T(8,128)(2,1)S(1)} %collective-permute-done.17.refs_1_), channel_id=1, source_target_pairs={{0,1},{1,3},{2,0},{3,2},{4,6},{5,4},{6,7},{7,5},{8,9},{9,11},{10,8... | collective-permute-start | bytes 798728 | tf_op jit(solution)/shard_map/ppermute | solution.py:203
  36.4 1.1 %collective-permute-start.21 = (bf16[1040,128]{1,0:T(8,128)(2,1)S(1)}, bf16[1040,128]{1,0:T(8,128)(2,1)S(1)}, u32[]{:S(2)}, u32[]{:S(2)}) collective-permute-start(bf16[1040,128]{1,0:T(8,128)(2,1)S(1)} %collective-permute-done.17.refs_1_), channel_id=1, source_target_pairs={{0,4},{1,5},{2,6},{3,7},{4,0},{5,1},{6,2},{7,3},{8,12},{9,13},{10,... | collective-permute-start | bytes 798728 | tf_op jit(solution)/shard_map/ppermute | solution.py:203
  37.6 0.5 collective-permute-done.1.refs_1_
  38.1 1.2 %collective-permute-start.10 = (bf16[1040,128]{1,0:T(8,128)(2,1)S(1)}, bf16[1040,128]{1,0:T(8,128)(2,1)S(1)}, u32[]{:S(2)}, u32[]{:S(2)}) collective-permute-start(bf16[1040,128]{1,0:T(8,128)(2,1)S(1)} %collective-permute-done.9.refs_1_), channel_id=1, source_target_pairs={{0,1},{1,3},{2,0},{3,2},{4,6},{5,4},{6,7},{7,5},{8,9},{9,11},{10,8... | collective-permute-start | bytes 798728 | tf_op jit(solution)/shard_map/ppermute | solution.py:203
  39.3 1.6 %collective-permute-done.26.refs_2_ = bf16[1040,128]{1,0:T(8,128)(2,1)S(1)} collective-permute-done((bf16[1040,128]{1,0:T(8,128)(2,1)S(1)}, bf16[1040,128]{1,0:T(8,128)(2,1)S(1)}, u32[]{:S(2)}, u32[]{:S(2)}) %collective-permute-start.26) | collective-permute-done | bytes 266272 | tf_op jit(solution)/shard_map/ppermute | solution.py:203
  40.9 0.9 collective-permute-start.13
  41.8 0.7 copy-done.12
  42.5 1.2 %collective-permute-start.2 = (bf16[1040,128]{1,0:T(8,128)(2,1)S(1)}, bf16[1040,128]{1,0:T(8,128)(2,1)S(1)}, u32[]{:S(2)}, u32[]{:S(2)}) collective-permute-start(bf16[1040,128]{1,0:T(8,128)(2,1)S(1)} %collective-permute-done.1.refs_1_), channel_id=1, source_target_pairs={{0,1},{1,3},{2,0},{3,2},{4,6},{5,4},{6,7},{7,5},{8,9},{9,11},{10,8... | collective-permute-start | bytes 798728 | tf_op jit(solution)/shard_map/ppermute | solution.py:203
  43.8 0.9 collective-permute-start.30
  44.7 0.7 copy-done.10
  45.4 1.2 %collective-permute-start.19 = (bf16[1040,128]{1,0:T(8,128)(2,1)S(1)}, bf16[1040,128]{1,0:T(8,128)(2,1)}, u32[]{:S(2)}, u32[]{:S(2)}) collective-permute-start(bf16[1040,128]{1,0:T(8,128)(2,1)S(1)} %collective-permute-done.18.refs_2_), channel_id=1, source_target_pairs={{0,1},{1,3},{2,0},{3,2},{4,6},{5,4},{6,7},{7,5},{8,9},{9,11},{10,8... | collective-permute-start | bytes 798728 | tf_op jit(solution)/shard_map/ppermute | solution.py:203
  46.6 1.2 %collective-permute-start.11 = (bf16[1040,128]{1,0:T(8,128)(2,1)S(1)}, bf16[1040,128]{1,0:T(8,128)(2,1)}, u32[]{:S(2)}, u32[]{:S(2)}) collective-permute-start(bf16[1040,128]{1,0:T(8,128)(2,1)S(1)} %collective-permute-done.10.refs_2_), channel_id=1, source_target_pairs={{0,1},{1,3},{2,0},{3,2},{4,6},{5,4},{6,7},{7,5},{8,9},{9,11},{10,8... | collective-permute-start | bytes 798728 | tf_op jit(solution)/shard_map/ppermute | solution.py:203
  47.9 1.1 %collective-permute-start.22 = (bf16[1040,128]{1,0:T(8,128)(2,1)S(1)}, bf16[1040,128]{1,0:T(8,128)(2,1)}, u32[]{:S(2)}, u32[]{:S(2)}) collective-permute-start(bf16[1040,128]{1,0:T(8,128)(2,1)S(1)} %collective-permute-done.18.refs_2_), channel_id=1, source_target_pairs={{0,4},{1,5},{2,6},{3,7},{4,0},{5,1},{6,2},{7,3},{8,12},{9,13},{10,... | collective-permute-start | bytes 798728 | tf_op jit(solution)/shard_map/ppermute | solution.py:203
  49.0 0.5 collective-permute-done.2.refs_2_
  49.5 0.9 collective-permute-start.14
  50.4 0.7 copy-done.14
  51.1 1.2 %collective-permute-start.3 = (bf16[1040,128]{1,0:T(8,128)(2,1)S(1)}, bf16[1040,128]{1,0:T(8,128)(2,1)}, u32[]{:S(2)}, u32[]{:S(2)}) collective-permute-start(bf16[1040,128]{1,0:T(8,128)(2,1)S(1)} %collective-permute-done.2.refs_2_), channel_id=1, source_target_pairs={{0,1},{1,3},{2,0},{3,2},{4,6},{5,4},{6,7},{7,5},{8,9},{9,11},{10,8... | collective-permute-start | bytes 798728 | tf_op jit(solution)/shard_map/ppermute | solution.py:203
  52.5 0.9 collective-permute-start.23
  53.3 0.7 slice.3
  54.1 1.2 %collective-permute-done.11.refs_3_ = bf16[1040,128]{1,0:T(8,128)(2,1)} collective-permute-done((bf16[1040,128]{1,0:T(8,128)(2,1)S(1)}, bf16[1040,128]{1,0:T(8,128)(2,1)}, u32[]{:S(2)}, u32[]{:S(2)}) %collective-permute-start.11) | collective-permute-done | bytes 266272 | tf_op jit(solution)/shard_map/ppermute | solution.py:203
  55.3 0.9 collective-permute-start.15
  56.2 1.4 %copy.18 = bf16[2,64,4,8,128]{4,3,1,2,0:T(8,128)(2,1)S(1)} copy(bf16[2,64,4,8,128]{4,3,2,1,0:T(8,128)(2,1)} %bitcast.15) | data formatting | bytes 2097152 | tf_op jit(solution)/shard_map/reshape | solution.py:228
  58.2 0.8 collective-permute-start.6
  59.1 0.9 %copy-done.15 = bf16[1040,128]{1,0:T(8,128)(2,1)S(1)} copy-done((bf16[1040,128]{1,0:T(8,128)(2,1)S(1)}, bf16[1040,128]{1,0:T(8,128)(2,1)}, u32[]{:S(2)}) %copy-start.15) | copy-done | bytes 266264
  60.0 6.3 %attend.4 = (f32[2,4,512,128]{3,2,1,0:T(8,128)S(1)}, f32[2,4,512,128]{3,2,1,0:T(8,128)S(1)}, f32[2,4,512,128]{3,2,1,0:T(8,128)S(1)}) custom-call(s32[2]{0:T(128)S(1)} %and_select_fusion.1.own_ids, bf16[2,4,512,128]{3,2,1,0:T(8,128)(2,1)S(1)} %bitcast.11, bf16[1040,128]{1,0:T(8,128)(2,1)S(1)} %copy-done.3, bf16[1040,128]{1,0:T(8,128)(2,1)S(1)} %copy-done.7, ...), custom_call_target="tpu_custom_call" | custom-call | flops 939524096 | bytes 8388608 | tf_op jit(solution)/shard_map/attend/pallas_call | solution.py:156
  66.4 6.5 %attend.5 = (f32[2,4,512,128]{3,2,1,0:T(8,128)S(1)}, f32[2,4,512,128]{3,2,1,0:T(8,128)S(1)}, f32[2,4,512,128]{3,2,1,0:T(8,128)S(1)}) custom-call(s32[2]{0:T(128)S(1)} %and_select_fusion.1.own_ids, bf16[2,4,512,128]{3,2,1,0:T(8,128)(2,1)S(1)} %bitcast.12, ...), custom_call_target="tpu_custom_call", output_to_operand_aliasing={{0}: (10, {}), {1}: (11, {}), {2}: (12, {})} | custom-call | flops 1073741824 | bytes 8388608 | tf_op jit(solution)/shard_map/attend/pallas_call | solution.py:156
  72.9 8.6 %attend.6 = (f32[2,4,512,128]{3,2,1,0:T(8,128)S(1)}, f32[2,4,512,128]{3,2,1,0:T(8,128)S(1)}, f32[2,4,512,128]{3,2,1,0:T(8,128)S(1)}) custom-call(s32[2]{0:T(128)S(1)} %and_select_fusion.1.own_ids, bf16[2,4,512,128]{3,2,1,0:T(8,128)(2,1)S(1)} %bitcast.13, ...), custom_call_target="tpu_custom_call", output_to_operand_aliasing={{0}: (10, {}), {1}: (11, {}), {2}: (12, {})} | custom-call | flops 1073741824 | bytes 8388608 | tf_op jit(solution)/shard_map/attend/pallas_call | solution.py:156
  81.6 8.2 %attend.7 = (bf16[128,32,128]{2,1,0:T(8,128)(2,1)}, f32[2,4,512,128]{3,2,1,0:T(8,128)S(1)}, f32[2,4,512,128]{3,2,1,0:T(8,128)S(1)}, f32[2,4,512,128]{3,2,1,0:T(8,128)S(1)}) custom-call(s32[2]{0:T(128)S(1)} %and_select_fusion.1.own_ids, bf16[2,4,512,128]{3,2,1,0:T(8,128)(2,1)S(1)} %bitcast.14, ...), custom_call_target="tpu_custom_call", output_to_operand_aliasing={{1}: (10, {}), {2}: (11, {}), {3}: (12, {})} | custom-call | flops 1073741824 | bytes 8388608 | tf_op jit(solution)/shard_map/attend/pallas_call | solution.py:156
  (59 shorter events, 1.9 us)
Async XLA Ops:
  2.6 5.6 %collective-permute-start.24 = (bf16[1040,128]{1,0:T(8,128)(2,1)S(1)}, bf16[1040,128]{1,0:T(8,128)(2,1)S(1)}, u32[]{:S(2)}, u32[]{:S(2)}) collective-permute-start(bf16[1040,128]{1,0:T(8,128)(2,1)S(1)} %pad_maximum_fusion.refs_7_), channel_id=1, source_target_pairs={{0,1},{1,3},{2,0},{3,2},{4,6},{5,4},{6,7},{7,5},{8,9},{9,11},{10,8... | collective-permute-start | bytes 798728 | tf_op jit(solution)/shard_map/ppermute | solution.py:203
  3.9 5.6 %collective-permute-start.27 = (bf16[1040,128]{1,0:T(8,128)(2,1)S(1)}, bf16[1040,128]{1,0:T(8,128)(2,1)S(1)}, u32[]{:S(2)}, u32[]{:S(2)}) collective-permute-start(bf16[1040,128]{1,0:T(8,128)(2,1)S(1)} %pad_maximum_fusion.refs_7_), channel_id=1, source_target_pairs={{0,4},{1,5},{2,6},{3,7},{4,0},{5,1},{6,2},{7,3},{8,12},{9,13},{10,... | collective-permute-start | bytes 798728 | tf_op jit(solution)/shard_map/ppermute | solution.py:203
  3.9 7.8 %collective-permute-start.16 = (bf16[1040,128]{1,0:T(8,128)(2,1)S(1)}, bf16[1040,128]{1,0:T(8,128)(2,1)S(1)}, u32[]{:S(2)}, u32[]{:S(2)}) collective-permute-start(bf16[1040,128]{1,0:T(8,128)(2,1)S(1)} %pad_maximum_fusion.refs_7_), channel_id=1, source_target_pairs={{0,8},{1,9},{2,10},{3,11},{4,12},{5,13},{6,14},{7,15},{8,16},{9,17... | collective-permute-start | bytes 798728 | tf_op jit(solution)/shard_map/ppermute | solution.py:203
  3.9 24.4 %collective-permute-start.8 = (bf16[1040,128]{1,0:T(8,128)(2,1)S(1)}, bf16[1040,128]{1,0:T(8,128)(2,1)S(1)}, u32[]{:S(2)}, u32[]{:S(2)}) collective-permute-start(bf16[1040,128]{1,0:T(8,128)(2,1)S(1)} %pad_maximum_fusion.refs_7_), channel_id=1, source_target_pairs={{0,16},{1,17},{2,18},{3,19},{4,20},{5,21},{6,22},{7,23},{8,24},{9,... | collective-permute-start | bytes 798728 | tf_op jit(solution)/shard_map/ppermute | solution.py:203
  5.2 24.5 %collective-permute-start = (bf16[1040,128]{1,0:T(8,128)(2,1)S(1)}, bf16[1040,128]{1,0:T(8,128)(2,1)S(1)}, u32[]{:S(2)}, u32[]{:S(2)}) collective-permute-start(bf16[1040,128]{1,0:T(8,128)(2,1)S(1)} %pad_maximum_fusion.refs_7_), channel_id=1, source_target_pairs={{0,24},{1,25},{2,26},{3,27},{4,28},{5,29},{6,30},{7,31},{8,0},{9,1... | collective-permute-start | bytes 798728 | tf_op jit(solution)/shard_map/ppermute | solution.py:203
  5.4 0.7 copy-start
  8.2 22.7 %collective-permute-start.25 = (bf16[1040,128]{1,0:T(8,128)(2,1)S(1)}, bf16[1040,128]{1,0:T(8,128)(2,1)S(1)}, u32[]{:S(2)}, u32[]{:S(2)}) collective-permute-start(bf16[1040,128]{1,0:T(8,128)(2,1)S(1)} %collective-permute-done.24.refs_0_), channel_id=1, source_target_pairs={{0,1},{1,3},{2,0},{3,2},{4,6},{5,4},{6,7},{7,5},{8,9},{9,11},{10,8... | collective-permute-start | bytes 798728 | tf_op jit(solution)/shard_map/ppermute | solution.py:203
  9.4 0.7 copy-start.4
  10.1 21.0 %collective-permute-start.28 = (bf16[1040,128]{1,0:T(8,128)(2,1)S(1)}, bf16[1040,128]{1,0:T(8,128)(2,1)S(1)}, u32[]{:S(2)}, u32[]{:S(2)}) collective-permute-start(bf16[1040,128]{1,0:T(8,128)(2,1)S(1)} %collective-permute-done.24.refs_0_), channel_id=1, source_target_pairs={{0,4},{1,5},{2,6},{3,7},{4,0},{5,1},{6,2},{7,3},{8,12},{9,13},{10,... | collective-permute-start | bytes 798728 | tf_op jit(solution)/shard_map/ppermute | solution.py:203
  11.0 0.7 copy-start.2
  11.7 21.2 %collective-permute-start.17 = (bf16[1040,128]{1,0:T(8,128)(2,1)S(1)}, bf16[1040,128]{1,0:T(8,128)(2,1)S(1)}, u32[]{:S(2)}, u32[]{:S(2)}) collective-permute-start(bf16[1040,128]{1,0:T(8,128)(2,1)S(1)} %collective-permute-done.16.refs_0_), channel_id=1, source_target_pairs={{0,1},{1,3},{2,0},{3,2},{4,6},{5,4},{6,7},{7,5},{8,9},{9,11},{10,8... | collective-permute-start | bytes 798728 | tf_op jit(solution)/shard_map/ppermute | solution.py:203
  28.3 5.0 %collective-permute-start.20 = (bf16[1040,128]{1,0:T(8,128)(2,1)S(1)}, bf16[1040,128]{1,0:T(8,128)(2,1)S(1)}, u32[]{:S(2)}, u32[]{:S(2)}) collective-permute-start(bf16[1040,128]{1,0:T(8,128)(2,1)S(1)} %collective-permute-done.16.refs_0_), channel_id=1, source_target_pairs={{0,4},{1,5},{2,6},{3,7},{4,0},{5,1},{6,2},{7,3},{8,12},{9,13},{10,... | collective-permute-start | bytes 798728 | tf_op jit(solution)/shard_map/ppermute | solution.py:203
  29.7 5.6 %collective-permute-start.9 = (bf16[1040,128]{1,0:T(8,128)(2,1)S(1)}, bf16[1040,128]{1,0:T(8,128)(2,1)S(1)}, u32[]{:S(2)}, u32[]{:S(2)}) collective-permute-start(bf16[1040,128]{1,0:T(8,128)(2,1)S(1)} %collective-permute-done.8.refs_0_), channel_id=1, source_target_pairs={{0,1},{1,3},{2,0},{3,2},{4,6},{5,4},{6,7},{7,5},{8,9},{9,11},{10,8... | collective-permute-start | bytes 798728 | tf_op jit(solution)/shard_map/ppermute | solution.py:203
  30.9 5.6 %collective-permute-start.12 = (bf16[1040,128]{1,0:T(8,128)(2,1)S(1)}, bf16[1040,128]{1,0:T(8,128)(2,1)S(1)}, u32[]{:S(2)}, u32[]{:S(2)}) collective-permute-start(bf16[1040,128]{1,0:T(8,128)(2,1)S(1)} %collective-permute-done.8.refs_0_), channel_id=1, source_target_pairs={{0,4},{1,5},{2,6},{3,7},{4,0},{5,1},{6,2},{7,3},{8,12},{9,13},{10,... | collective-permute-start | bytes 798728 | tf_op jit(solution)/shard_map/ppermute | solution.py:203
  31.1 0.7 copy-start.8
  31.9 6.2 %collective-permute-start.1 = (bf16[1040,128]{1,0:T(8,128)(2,1)S(1)}, bf16[1040,128]{1,0:T(8,128)(2,1)S(1)}, u32[]{:S(2)}, u32[]{:S(2)}) collective-permute-start(bf16[1040,128]{1,0:T(8,128)(2,1)S(1)} %collective-permute-done.refs_0_), channel_id=1, source_target_pairs={{0,1},{1,3},{2,0},{3,2},{4,6},{5,4},{6,7},{7,5},{8,9},{9,11},{10,8... | collective-permute-start | bytes 798728 | tf_op jit(solution)/shard_map/ppermute | solution.py:203
  32.8 8.1 %collective-permute-start.26 = (bf16[1040,128]{1,0:T(8,128)(2,1)S(1)}, bf16[1040,128]{1,0:T(8,128)(2,1)S(1)}, u32[]{:S(2)}, u32[]{:S(2)}) collective-permute-start(bf16[1040,128]{1,0:T(8,128)(2,1)S(1)} %collective-permute-done.25.refs_1_), channel_id=1, source_target_pairs={{0,1},{1,3},{2,0},{3,2},{4,6},{5,4},{6,7},{7,5},{8,9},{9,11},{10,8... | collective-permute-start | bytes 798728 | tf_op jit(solution)/shard_map/ppermute | solution.py:203
  33.4 8.5 %collective-permute-start.29 = (bf16[1040,128]{1,0:T(8,128)(2,1)S(1)}, bf16[1040,128]{1,0:T(8,128)(2,1)S(1)}, u32[]{:S(2)}, u32[]{:S(2)}) collective-permute-start(bf16[1040,128]{1,0:T(8,128)(2,1)S(1)} %collective-permute-done.25.refs_1_), channel_id=1, source_target_pairs={{0,4},{1,5},{2,6},{3,7},{4,0},{5,1},{6,2},{7,3},{8,12},{9,13},{10,... | collective-permute-start | bytes 798728 | tf_op jit(solution)/shard_map/ppermute | solution.py:203
  34.1 0.7 copy-start.6
  35.2 8.6 %collective-permute-start.18 = (bf16[1040,128]{1,0:T(8,128)(2,1)S(1)}, bf16[1040,128]{1,0:T(8,128)(2,1)S(1)}, u32[]{:S(2)}, u32[]{:S(2)}) collective-permute-start(bf16[1040,128]{1,0:T(8,128)(2,1)S(1)} %collective-permute-done.17.refs_1_), channel_id=1, source_target_pairs={{0,1},{1,3},{2,0},{3,2},{4,6},{5,4},{6,7},{7,5},{8,9},{9,11},{10,8... | collective-permute-start | bytes 798728 | tf_op jit(solution)/shard_map/ppermute | solution.py:203
  36.4 8.9 %collective-permute-start.21 = (bf16[1040,128]{1,0:T(8,128)(2,1)S(1)}, bf16[1040,128]{1,0:T(8,128)(2,1)S(1)}, u32[]{:S(2)}, u32[]{:S(2)}) collective-permute-start(bf16[1040,128]{1,0:T(8,128)(2,1)S(1)} %collective-permute-done.17.refs_1_), channel_id=1, source_target_pairs={{0,4},{1,5},{2,6},{3,7},{4,0},{5,1},{6,2},{7,3},{8,12},{9,13},{10,... | collective-permute-start | bytes 798728 | tf_op jit(solution)/shard_map/ppermute | solution.py:203
  38.1 8.6 %collective-permute-start.10 = (bf16[1040,128]{1,0:T(8,128)(2,1)S(1)}, bf16[1040,128]{1,0:T(8,128)(2,1)S(1)}, u32[]{:S(2)}, u32[]{:S(2)}) collective-permute-start(bf16[1040,128]{1,0:T(8,128)(2,1)S(1)} %collective-permute-done.9.refs_1_), channel_id=1, source_target_pairs={{0,1},{1,3},{2,0},{3,2},{4,6},{5,4},{6,7},{7,5},{8,9},{9,11},{10,8... | collective-permute-start | bytes 798728 | tf_op jit(solution)/shard_map/ppermute | solution.py:203
  40.9 6.9 %collective-permute-start.13 = (bf16[1040,128]{1,0:T(8,128)(2,1)S(1)}, bf16[1040,128]{1,0:T(8,128)(2,1)S(1)}, u32[]{:S(2)}, u32[]{:S(2)}) collective-permute-start(bf16[1040,128]{1,0:T(8,128)(2,1)S(1)} %collective-permute-done.9.refs_1_), channel_id=1, source_target_pairs={{0,4},{1,5},{2,6},{3,7},{4,0},{5,1},{6,2},{7,3},{8,12},{9,13},{10,... | collective-permute-start | bytes 798728 | tf_op jit(solution)/shard_map/ppermute | solution.py:203
  41.8 0.7 copy-start.12
  42.5 7.0 %collective-permute-start.2 = (bf16[1040,128]{1,0:T(8,128)(2,1)S(1)}, bf16[1040,128]{1,0:T(8,128)(2,1)S(1)}, u32[]{:S(2)}, u32[]{:S(2)}) collective-permute-start(bf16[1040,128]{1,0:T(8,128)(2,1)S(1)} %collective-permute-done.1.refs_1_), channel_id=1, source_target_pairs={{0,1},{1,3},{2,0},{3,2},{4,6},{5,4},{6,7},{7,5},{8,9},{9,11},{10,8... | collective-permute-start | bytes 798728 | tf_op jit(solution)/shard_map/ppermute | solution.py:203
  43.8 6.6 %collective-permute-start.30 = (bf16[1040,128]{1,0:T(8,128)(2,1)S(1)}, bf16[1040,128]{1,0:T(8,128)(2,1)S(1)}, u32[]{:S(2)}, u32[]{:S(2)}) collective-permute-start(bf16[1040,128]{1,0:T(8,128)(2,1)S(1)} %collective-permute-done.26.refs_2_), channel_id=1, source_target_pairs={{0,4},{1,5},{2,6},{3,7},{4,0},{5,1},{6,2},{7,3},{8,12},{9,13},{10,... | collective-permute-start | bytes 798728 | tf_op jit(solution)/shard_map/ppermute | solution.py:203
  44.7 0.7 copy-start.10
  45.4 7.1 %collective-permute-start.19 = (bf16[1040,128]{1,0:T(8,128)(2,1)S(1)}, bf16[1040,128]{1,0:T(8,128)(2,1)}, u32[]{:S(2)}, u32[]{:S(2)}) collective-permute-start(bf16[1040,128]{1,0:T(8,128)(2,1)S(1)} %collective-permute-done.18.refs_2_), channel_id=1, source_target_pairs={{0,1},{1,3},{2,0},{3,2},{4,6},{5,4},{6,7},{7,5},{8,9},{9,11},{10,8... | collective-permute-start | bytes 798728 | tf_op jit(solution)/shard_map/ppermute | solution.py:203
  46.6 8.7 %collective-permute-start.11 = (bf16[1040,128]{1,0:T(8,128)(2,1)S(1)}, bf16[1040,128]{1,0:T(8,128)(2,1)}, u32[]{:S(2)}, u32[]{:S(2)}) collective-permute-start(bf16[1040,128]{1,0:T(8,128)(2,1)S(1)} %collective-permute-done.10.refs_2_), channel_id=1, source_target_pairs={{0,1},{1,3},{2,0},{3,2},{4,6},{5,4},{6,7},{7,5},{8,9},{9,11},{10,8... | collective-permute-start | bytes 798728 | tf_op jit(solution)/shard_map/ppermute | solution.py:203
  47.9 9.7 %collective-permute-start.22 = (bf16[1040,128]{1,0:T(8,128)(2,1)S(1)}, bf16[1040,128]{1,0:T(8,128)(2,1)}, u32[]{:S(2)}, u32[]{:S(2)}) collective-permute-start(bf16[1040,128]{1,0:T(8,128)(2,1)S(1)} %collective-permute-done.18.refs_2_), channel_id=1, source_target_pairs={{0,4},{1,5},{2,6},{3,7},{4,0},{5,1},{6,2},{7,3},{8,12},{9,13},{10,... | collective-permute-start | bytes 798728 | tf_op jit(solution)/shard_map/ppermute | solution.py:203
  49.5 8.2 %collective-permute-start.14 = (bf16[1040,128]{1,0:T(8,128)(2,1)S(1)}, bf16[1040,128]{1,0:T(8,128)(2,1)}, u32[]{:S(2)}, u32[]{:S(2)}) collective-permute-start(bf16[1040,128]{1,0:T(8,128)(2,1)S(1)} %collective-permute-done.10.refs_2_), channel_id=1, source_target_pairs={{0,4},{1,5},{2,6},{3,7},{4,0},{5,1},{6,2},{7,3},{8,12},{9,13},{10,... | collective-permute-start | bytes 798728 | tf_op jit(solution)/shard_map/ppermute | solution.py:203
  50.4 0.7 copy-start.14
  51.1 7.1 %collective-permute-start.3 = (bf16[1040,128]{1,0:T(8,128)(2,1)S(1)}, bf16[1040,128]{1,0:T(8,128)(2,1)}, u32[]{:S(2)}, u32[]{:S(2)}) collective-permute-start(bf16[1040,128]{1,0:T(8,128)(2,1)S(1)} %collective-permute-done.2.refs_2_), channel_id=1, source_target_pairs={{0,1},{1,3},{2,0},{3,2},{4,6},{5,4},{6,7},{7,5},{8,9},{9,11},{10,8... | collective-permute-start | bytes 798728 | tf_op jit(solution)/shard_map/ppermute | solution.py:203
  52.5 6.6 %collective-permute-start.23 = (bf16[1040,128]{1,0:T(8,128)(2,1)}, bf16[1040,128]{1,0:T(8,128)(2,1)}, u32[]{:S(2)}, u32[]{:S(2)}) collective-permute-start(bf16[1040,128]{1,0:T(8,128)(2,1)} %collective-permute-done.19.refs_3_), channel_id=1, source_target_pairs={{0,4},{1,5},{2,6},{3,7},{4,0},{5,1},{6,2},{7,3},{8,12},{9,13},{10,... | collective-permute-start | bytes 798728 | tf_op jit(solution)/shard_map/ppermute | solution.py:203
  54.1 5.0 %copy-start.1 = (bf16[1040,128]{1,0:T(8,128)(2,1)S(1)}, bf16[1040,128]{1,0:T(8,128)(2,1)}, u32[]{:S(2)}) copy-start(bf16[1040,128]{1,0:T(8,128)(2,1)} %copy-done) | copy-start | bytes 798724
  54.1 5.0 %copy-start.3 = (bf16[1040,128]{1,0:T(8,128)(2,1)S(1)}, bf16[1040,128]{1,0:T(8,128)(2,1)}, u32[]{:S(2)}) copy-start(bf16[1040,128]{1,0:T(8,128)(2,1)} %copy-done.2) | copy-start | bytes 798724
  54.1 5.0 %copy-start.5 = (bf16[1040,128]{1,0:T(8,128)(2,1)S(1)}, bf16[1040,128]{1,0:T(8,128)(2,1)}, u32[]{:S(2)}) copy-start(bf16[1040,128]{1,0:T(8,128)(2,1)} %copy-done.4) | copy-start | bytes 798724
  54.1 5.0 %copy-start.7 = (bf16[1040,128]{1,0:T(8,128)(2,1)S(1)}, bf16[1040,128]{1,0:T(8,128)(2,1)}, u32[]{:S(2)}) copy-start(bf16[1040,128]{1,0:T(8,128)(2,1)} %copy-done.6) | copy-start | bytes 798724
  54.1 5.0 %copy-start.9 = (bf16[1040,128]{1,0:T(8,128)(2,1)S(1)}, bf16[1040,128]{1,0:T(8,128)(2,1)}, u32[]{:S(2)}) copy-start(bf16[1040,128]{1,0:T(8,128)(2,1)} %copy-done.8) | copy-start | bytes 798724
  54.1 5.0 %copy-start.11 = (bf16[1040,128]{1,0:T(8,128)(2,1)S(1)}, bf16[1040,128]{1,0:T(8,128)(2,1)}, u32[]{:S(2)}) copy-start(bf16[1040,128]{1,0:T(8,128)(2,1)} %copy-done.10) | copy-start | bytes 798724
  54.1 5.0 %copy-start.13 = (bf16[1040,128]{1,0:T(8,128)(2,1)S(1)}, bf16[1040,128]{1,0:T(8,128)(2,1)}, u32[]{:S(2)}) copy-start(bf16[1040,128]{1,0:T(8,128)(2,1)} %copy-done.12) | copy-start | bytes 798724
  55.3 17.6 %collective-permute-start.15 = (bf16[1040,128]{1,0:T(8,128)(2,1)}, bf16[1040,128]{1,0:T(8,128)(2,1)S(1)}, u32[]{:S(2)}, u32[]{:S(2)}) collective-permute-start(bf16[1040,128]{1,0:T(8,128)(2,1)} %collective-permute-done.11.refs_3_), channel_id=1, source_target_pairs={{0,4},{1,5},{2,6},{3,7},{4,0},{5,1},{6,2},{7,3},{8,12},{9,13},{10,... | collective-permute-start | bytes 798728 | tf_op jit(solution)/shard_map/ppermute | solution.py:203
  57.6 23.9 %collective-permute-start.4 = (bf16[1040,128]{1,0:T(8,128)(2,1)S(1)}, bf16[1040,128]{1,0:T(8,128)(2,1)S(1)}, u32[]{:S(2)}, u32[]{:S(2)}) collective-permute-start(bf16[1040,128]{1,0:T(8,128)(2,1)S(1)} %collective-permute-done.refs_0_), channel_id=1, source_target_pairs={{0,4},{1,5},{2,6},{3,7},{4,0},{5,1},{6,2},{7,3},{8,12},{9,13},{10,... | collective-permute-start | bytes 798728 | tf_op jit(solution)/shard_map/ppermute | solution.py:203
  57.7 23.9 %collective-permute-start.5 = (bf16[1040,128]{1,0:T(8,128)(2,1)S(1)}, bf16[1040,128]{1,0:T(8,128)(2,1)S(1)}, u32[]{:S(2)}, u32[]{:S(2)}) collective-permute-start(bf16[1040,128]{1,0:T(8,128)(2,1)S(1)} %collective-permute-done.1.refs_1_), channel_id=1, source_target_pairs={{0,4},{1,5},{2,6},{3,7},{4,0},{5,1},{6,2},{7,3},{8,12},{9,13},{10,... | collective-permute-start | bytes 798728 | tf_op jit(solution)/shard_map/ppermute | solution.py:203
  58.2 23.4 %collective-permute-start.6 = (bf16[1040,128]{1,0:T(8,128)(2,1)S(1)}, bf16[1040,128]{1,0:T(8,128)(2,1)S(1)}, u32[]{:S(2)}, u32[]{:S(2)}) collective-permute-start(bf16[1040,128]{1,0:T(8,128)(2,1)S(1)} %collective-permute-done.2.refs_2_), channel_id=1, source_target_pairs={{0,4},{1,5},{2,6},{3,7},{4,0},{5,1},{6,2},{7,3},{8,12},{9,13},{10,... | collective-permute-start | bytes 798728 | tf_op jit(solution)/shard_map/ppermute | solution.py:203
  59.0 22.5 %collective-permute-start.7 = (bf16[1040,128]{1,0:T(8,128)(2,1)}, bf16[1040,128]{1,0:T(8,128)(2,1)S(1)}, u32[]{:S(2)}, u32[]{:S(2)}) collective-permute-start(bf16[1040,128]{1,0:T(8,128)(2,1)} %collective-permute-done.3.refs_3_), channel_id=1, source_target_pairs={{0,4},{1,5},{2,6},{3,7},{4,0},{5,1},{6,2},{7,3},{8,12},{9,13},{10,... | collective-permute-start | bytes 798728 | tf_op jit(solution)/shard_map/ppermute | solution.py:203
  59.1 1.0 %copy-start.15 = (bf16[1040,128]{1,0:T(8,128)(2,1)S(1)}, bf16[1040,128]{1,0:T(8,128)(2,1)}, u32[]{:S(2)}) copy-start(bf16[1040,128]{1,0:T(8,128)(2,1)} %copy-done.14) | copy-start | bytes 798724

commit v2 on v1

--- a/solution.py
+++ b/solution.py
@@ -44,16 +44,16 @@
     heads_kv = q_ref.shape[1]
     rows = q_ref.shape[2]
     run_rows = 2 * heads_kv * RUN
-    kv_refs, refs = refs[:blocks], refs[blocks:]
-    if first:
-        own_ref, refs = refs[0], refs[1:]
-    else:
+    block_rows = 2 * run_rows + 16
+    kv_refs, refs = refs[: len(blocks)], refs[len(blocks) :]
+    if not first:
         refs = refs[3:]
     if last:
         out_ref, refs = refs[0], refs[1:]
     top_ref, total_ref, mixed_ref, buf = refs
 
     if first:
+        own_ref = kv_refs[0]
         row_at = lax.broadcasted_iota(jnp.int32, (rows, 2 * RUN), 0) // group
         col_at = lax.broadcasted_iota(jnp.int32, (rows, 2 * RUN), 1)
         for a in range(2):
@@ -83,10 +83,18 @@
                     factor,
                 )
 
+    every = [
+        (ref, n * block_rows)
+        for at, ref in enumerate(kv_refs)
+        for n in range(blocks[at])
+        if not (first and at == 0 and n == 0)
+    ]
     flags = [[], []]
-    for start in range(0, blocks, 8):
-        some = kv_refs[start : start + 8]
-        ids = jnp.concatenate([ref[2 * run_rows :] for ref in some]).astype(jnp.float32)
+    for start in range(0, len(every), 8):
+        some = every[start : start + 8]
+        ids = jnp.concatenate(
+            [ref[at + 2 * run_rows : at + block_rows] for ref, at in some]
+        ).astype(jnp.float32)
         row = lax.broadcasted_iota(jnp.int32, ids.shape, 0)
         lane = lax.broadcasted_iota(jnp.int32, ids.shape, 1)
         bit = jnp.left_shift(1, 2 * (row // 16) + lane // RUN)
@@ -101,12 +109,13 @@
     col = lax.broadcasted_iota(jnp.int32, (8, TILE * RUN), 1)
     for a in range(2):
         count = jnp.int32(0)
-        for n in range(2 * blocks):
+        for n in range(2 * len(every)):
 
             @pl.when(flags[a][n] == 1)
             def _():
-                at = (n % 2) * run_rows
-                buf[a, count] = kv_refs[n // 2][at : at + run_rows]
+                ref, at = every[n // 2]
+                at += (n % 2) * run_rows
+                buf[a, count] = ref[at : at + run_rows]
 
             count = count + flags[a][n]
         for s in range(TILE - 1):
@@ -142,17 +151,19 @@
                 )
 
 
-def attend(own_ids, q, kvs, own, state, out, group, half, factor):
-    first, last, blocks = own is not None, out is not None, len(kvs)
-    operands = [q, *kvs] + ([own] if first else list(state))
+def attend(own_ids, q, kvs, state, out, group, half, factor):
+    first, last = state is None, out is not None
+    run_rows = 2 * q.shape[1] * RUN
+    blocks = [x.shape[0] // (2 * run_rows + 16) for x in kvs]
+    count = sum(blocks) - int(first)
+    operands = [q, *kvs] + ([] if first else list(state))
     lanes = jax.ShapeDtypeStruct(q.shape[:3] + (128,), jnp.float32)
     carried = [lanes, lanes, jax.ShapeDtypeStruct(q.shape, jnp.float32)]
     vmem = pl.BlockSpec(memory_space=pltpu.VMEM)
     shapes = ([out] if last else []) + carried
     aliases = {}
     if not first:
-        aliases = {2 + blocks + n: int(last) + n for n in range(3)}
-    run_rows = 2 * q.shape[1] * RUN
+        aliases = {2 + len(kvs) + n: int(last) + n for n in range(3)}
     results = pl.pallas_call(
         functools.partial(attend_kernel, group, factor, half, first, last, blocks),
         out_shape=shapes,
@@ -162,13 +173,13 @@
             in_specs=[vmem] * len(operands),
             out_specs=[vmem] * len(shapes),
             scratch_shapes=[
-                pltpu.VMEM((2, 2 * blocks + TILE - 1, run_rows, q.shape[3]), q.dtype)
+                pltpu.VMEM((2, 2 * count + TILE - 1, run_rows, q.shape[3]), q.dtype)
             ],
         ),
         input_output_aliases=aliases,
         compiler_params=pltpu.CompilerParams(vmem_limit_bytes=24 * 1024 * 1024),
         cost_estimate=pl.CostEstimate(
-            flops=blocks * RUN * q.size * 4, bytes_accessed=q.size * 16, transcendentals=0
+            flops=count * RUN * q.size * 4, bytes_accessed=q.size * 16, transcendentals=0
         ),
         name="attend",
     )(own_ids, *operands)
@@ -184,9 +195,10 @@
     factor = math.log2(math.e) / math.sqrt(head_dim)
 
     chips = outer // 2
-    ring = list(range(inner // 2)) + list(range(inner - 1, inner // 2 - 1, -1))
-    after = {ring[n]: ring[(n + 1) % inner] for n in range(inner)}
-    before = {there: here for here, there in after.items()}
+    bits = inner.bit_length() - 1
+    ring = list(range(0, chips, 2))[:1] + list(range(1, chips, 2))
+    ring += list(range(2, chips, 2))[::-1]
+    after = {ring[n]: ring[(n + 1) % chips] for n in range(chips)}
 
     def permute(x, to):
         pairs = []
@@ -202,13 +214,19 @@
                     )
         return lax.ppermute(x, AXES, pairs)
 
-    def along_z(x, step):
-        return permute(x, lambda z, core, place: ((z + step) % chips, core, place))
-
-    def around(x):
-        return permute(
-            x, lambda z, core, place: (z, core, (before if core else after)[place])
+    def along_z(x):
+        return permute(x, lambda z, core, place: (after[z], core, place))
+
+    def doubled(x, step):
+        there = permute(
+            x,
+            lambda z, core, place: (
+                z,
+                core,
+                place ^ (1 << (bits - 1 - step if core else step)),
+            ),
         )
+        return jnp.concatenate([x, there])
 
     def other_core(x):
         return permute(x, lambda z, core, place: (z, 1 - core, place))
@@ -230,27 +248,21 @@
         .reshape(2, heads_kv, RUN * group, head_dim)
     )
 
-    starts = [own] + [along_z(own, step) for step in range(1, chips)]
-    state = None
-    for n, start in enumerate(starts):
-        mine = [start]
-        for _ in range(inner - 1):
-            mine.append(around(mine[-1]))
-        theirs = [other_core(x) for x in mine]
-        kvs = mine[1:] + theirs if n == 0 else mine + theirs
-        last = n == chips - 1
-        state = attend(
-            own_ids,
-            q,
-            kvs,
-            own if n == 0 else None,
-            state,
-            jax.ShapeDtypeStruct(queries.shape, queries.dtype) if last else None,
-            group,
-            half,
-            factor,
-        )
-    return state
+    stage = own
+    state, waiting = None, None
+    shape = jax.ShapeDtypeStruct(queries.shape, queries.dtype)
+
+    for n in range(chips):
+        later = along_z(stage) if n + 1 < chips else None
+        held = stage
+        for step in range(bits):
+            held = doubled(held, step)
+        if waiting is not None:
+            state = attend(own_ids, q, waiting, state, None, group, half, factor)
+            held, *state = lax.optimization_barrier((held, *state))
+        waiting = [held, other_core(held)]
+        stage = later
+    return attend(own_ids, q, waiting, state, shape, group, half, factor)
 
 
 def solution(mesh):

time: 89.5 us -> 67.5 us (0.75)
  the two profiles are of different devices: /device:TPU:29 before, /device:TPU:24 now
where the time goes in v2:
time: 67.5 us; the launch traced here: 68 us
  waiting for transfers between devices  28.7 us (43%)
  Pallas kernels  24 us (36%)
  starting transfers between devices  11.7 us (17%)
  local copies, waits for them, and re-layouts  2.14 us (3%)
  other arithmetic  1.21 us (2%)
    ppermute x15, waiting for transfers between devices, permute(): return lax.ppermute(x, AXES, pairs)  28.7 us
    pallas_call x4, Pallas kernels, attend(): pl.pallas_call(functools.partial(attend_kernel, group, factor, half, firs...  24 us
    ppermute x15, starting transfers between devices, permute(): return lax.ppermute(x, AXES, pairs)  11.7 us
    reshape x2, local copies, waits for them, and re-layouts, per_device(): x.reshape(2, RUN, heads_kv, head_dim)  1.85 us
  transfers between devices with their start and end apart: 15, of which 8 were waited for; matrix products, arithmetic and copies ran while one was open for 1% of the time, Pallas kernels for 14%

profile of v2, /device:TPU:24, one launch (start us, length us, event | category | flops | bytes accessed | tf_op | source)
XLA Modules:
  0.0 68.0 jit_solution(3475741798552810505)
XLA Ops:
  0.0 0.9 %copy.15 = bf16[2,64,4,128]{3,1,2,0:T(8,128)(2,1)S(1)} copy(bf16[2,64,4,128]{3,2,1,0:T(4,128)(2,1)} %bitcast.19) | data formatting | bytes 262144 | tf_op jit(solution)/shard_map/reshape | solution.py:235
  0.9 0.9 %copy.16 = bf16[2,64,4,128]{3,1,2,0:T(8,128)(2,1)S(1)} copy(bf16[2,64,4,128]{3,2,1,0:T(4,128)(2,1)} %bitcast.20) | data formatting | bytes 262144 | tf_op jit(solution)/shard_map/reshape | solution.py:235
  1.9 0.0 copy-start.1
  1.9 0.7 %fusion = bf16[128]{0:T(256)(128)(2,1)S(1)} fusion(s32[128]{0:T(128)} %param.7), kind=kLoop, calls=%fused_computation.19 | loop fusion | flops 2048 | bytes 768 | tf_op jit(solution)/shard_map/convert_element_type | solution.py:237
  2.6 0.0 copy-start
  2.7 0.5 collective-permute-start
  3.2 1.5 %collective-permute-start.9 = (bf16[1040,128]{1,0:T(8,128)(2,1)S(1)}, bf16[1040,128]{1,0:T(8,128)(2,1)S(1)}, u32[]{:S(2)}, u32[]{:S(2)}) collective-permute-start(bf16[1040,128]{1,0:T(8,128)(2,1)S(1)} %pad_maximum_fusion.8), channel_id=1, source_target_pairs={{0,1},{1,0},{2,3},{3,2},{4,6},{5,7},{6,4},{7,5},{8,9},{9,8},{10,11... | collective-permute-start | bytes 798728 | tf_op jit(solution)/shard_map/ppermute | solution.py:215
  4.7 7.1 %collective-permute-done = bf16[1040,128]{1,0:T(8,128)(2,1)S(1)} collective-permute-done((bf16[1040,128]{1,0:T(8,128)(2,1)S(1)}, bf16[1040,128]{1,0:T(8,128)(2,1)S(1)}, u32[]{:S(2)}, u32[]{:S(2)}) %collective-permute-start) | collective-permute-done | bytes 266272 | tf_op jit(solution)/shard_map/ppermute | solution.py:215
  11.8 1.5 %collective-permute-start.7 = (bf16[1040,128]{1,0:T(8,128)(2,1)S(1)}, bf16[1040,128]{1,0:T(8,128)(2,1)S(1)}, u32[]{:S(2)}, u32[]{:S(2)}) collective-permute-start(bf16[1040,128]{1,0:T(8,128)(2,1)S(1)} %collective-permute-done), channel_id=1, source_target_pairs={{0,1},{1,0},{2,3},{3,2},{4,6},{5,7},{6,4},{7,5},{8,9},{9,8},{10,11... | collective-permute-start | bytes 798728 | tf_op jit(solution)/shard_map/ppermute | solution.py:215
  13.3 0.0 collective-permute-done.9
  13.3 1.6 %collective-permute-start.10 = (bf16[2080,128]{1,0:T(8,128)(2,1)S(1)}, bf16[2080,128]{1,0:T(8,128)(2,1)S(1)}, u32[]{:S(2)}, u32[]{:S(2)}) collective-permute-start(bf16[2080,128]{1,0:T(8,128)(2,1)S(1)} %pad_maximum_fusion.7), channel_id=1, source_target_pairs={{0,2},{1,3},{2,0},{3,1},{4,5},{5,4},{6,7},{7,6},{8,10},{9,11},{10,... | collective-permute-start | bytes 1597448 | tf_op jit(solution)/shard_map/ppermute | solution.py:215
  14.9 0.0 copy-done.1
  14.9 0.1 slice.3
  15.0 0.0 copy-done
  15.0 0.2 copy.18
  15.2 0.1 collective-permute-start.1
  15.2 5.8 %collective-permute-done.7 = bf16[1040,128]{1,0:T(8,128)(2,1)S(1)} collective-permute-done((bf16[1040,128]{1,0:T(8,128)(2,1)S(1)}, bf16[1040,128]{1,0:T(8,128)(2,1)S(1)}, u32[]{:S(2)}, u32[]{:S(2)}) %collective-permute-start.7) | collective-permute-done | bytes 266272 | tf_op jit(solution)/shard_map/ppermute | solution.py:215
  21.0 1.7 %collective-permute-start.8 = (bf16[2080,128]{1,0:T(8,128)(2,1)S(1)}, bf16[2080,128]{1,0:T(8,128)(2,1)S(1)}, u32[]{:S(2)}, u32[]{:S(2)}) collective-permute-start(bf16[2080,128]{1,0:T(8,128)(2,1)S(1)} %pad_maximum_fusion.6), channel_id=1, source_target_pairs={{0,2},{1,3},{2,0},{3,1},{4,5},{5,4},{6,7},{7,6},{8,10},{9,11},{10,... | collective-permute-start | bytes 1597448 | tf_op jit(solution)/shard_map/ppermute | solution.py:215
  22.7 0.1 collective-permute-done.1
  22.8 1.4 %collective-permute-start.5 = (bf16[1040,128]{1,0:T(8,128)(2,1)S(1)}, bf16[1040,128]{1,0:T(8,128)(2,1)S(1)}, u32[]{:S(2)}, u32[]{:S(2)}) collective-permute-start(bf16[1040,128]{1,0:T(8,128)(2,1)S(1)} %collective-permute-done.1), channel_id=1, source_target_pairs={{0,1},{1,0},{2,3},{3,2},{4,6},{5,7},{6,4},{7,5},{8,9},{9,8},{10,11... | collective-permute-start | bytes 798728 | tf_op jit(solution)/shard_map/ppermute | solution.py:215
  24.2 0.0 collective-permute-done.10
  24.2 0.1 pad_maximum_fusion.3.refs_0_
  24.3 0.1 collective-permute-start.11
  24.4 0.1 collective-permute-start.2
  24.4 7.7 %collective-permute-done.5 = bf16[1040,128]{1,0:T(8,128)(2,1)S(1)} collective-permute-done((bf16[1040,128]{1,0:T(8,128)(2,1)S(1)}, bf16[1040,128]{1,0:T(8,128)(2,1)S(1)}, u32[]{:S(2)}, u32[]{:S(2)}) %collective-permute-start.5) | collective-permute-done | bytes 266272 | tf_op jit(solution)/shard_map/ppermute | solution.py:215
  32.2 0.6 collective-permute-start.6
  32.8 1.4 %collective-permute-done.2 = bf16[1040,128]{1,0:T(8,128)(2,1)S(1)} collective-permute-done((bf16[1040,128]{1,0:T(8,128)(2,1)S(1)}, bf16[1040,128]{1,0:T(8,128)(2,1)S(1)}, u32[]{:S(2)}, u32[]{:S(2)}) %collective-permute-start.2) | collective-permute-done | bytes 266272 | tf_op jit(solution)/shard_map/ppermute | solution.py:215
  34.1 0.6 collective-permute-start.3
  34.8 0.0 collective-permute-done.8
  34.8 0.1 pad_maximum_fusion.2.refs_0_
  34.8 0.0 collective-permute-done.11.refs_1_
  34.8 6.3 %attend.4 = (f32[2,4,512,128]{3,2,1,0:T(8,128)S(1)}, f32[2,4,512,128]{3,2,1,0:T(8,128)S(1)}, f32[2,4,512,128]{3,2,1,0:T(8,128)S(1)}) custom-call(s32[2]{0:T(128)S(1)} %and_select_fusion.1.own_ids, bf16[2,4,512,128]{3,2,1,0:T(8,128)(2,1)S(1)} %bitcast.11, bf16[4160,128]{1,0:T(8,128)(2,1)S(1)} %pad_maximum_fusion.3.refs_0_, ...), custom_call_target="tpu_custom_call" | custom-call | flops 939524096 | bytes 8388608 | tf_op jit(solution)/shard_map/attend/pallas_call | solution.py:167
  41.1 0.1 collective-permute-start.12
  41.2 0.0 collective-permute-done.3
  41.3 1.0 %collective-permute-start.4 = (bf16[2080,128]{1,0:T(8,128)(2,1)S(1)}, bf16[2080,128]{1,0:T(8,128)(2,1)S(1)}, u32[]{:S(2)}, u32[]{:S(2)}) collective-permute-start(bf16[2080,128]{1,0:T(8,128)(2,1)S(1)} %pad_maximum_fusion.4), channel_id=1, source_target_pairs={{0,2},{1,3},{2,0},{3,1},{4,5},{5,4},{6,7},{7,6},{8,10},{9,11},{10,... | collective-permute-start | bytes 1597448 | tf_op jit(solution)/shard_map/ppermute | solution.py:215
  42.3 2.1 %collective-permute-done.6 = bf16[2080,128]{1,0:T(8,128)(2,1)S(1)} collective-permute-done((bf16[2080,128]{1,0:T(8,128)(2,1)S(1)}, bf16[2080,128]{1,0:T(8,128)(2,1)S(1)}, u32[]{:S(2)}, u32[]{:S(2)}) %collective-permute-start.6) | collective-permute-done | bytes 532512 | tf_op jit(solution)/shard_map/ppermute | solution.py:215
  44.4 0.1 pad_maximum_fusion.1.refs_0_
  44.4 0.0 collective-permute-done.12.refs_1_
  44.5 3.2 %attend.5 = (f32[2,4,512,128]{3,2,1,0:T(8,128)S(1)}, f32[2,4,512,128]{3,2,1,0:T(8,128)S(1)}, f32[2,4,512,128]{3,2,1,0:T(8,128)S(1)}) custom-call(s32[2]{0:T(128)S(1)} %and_select_fusion.1.own_ids, bf16[2,4,512,128]{3,2,1,0:T(8,128)(2,1)S(1)} %bitcast.12, ...), custom_call_target="tpu_custom_call", output_to_operand_aliasing={{0}: (4, {}), {1}: (5, {}), {2}: (6, {})} | custom-call | flops 1073741824 | bytes 8388608 | tf_op jit(solution)/shard_map/attend/pallas_call | solution.py:167
  47.6 0.7 %collective-permute-start.13 = (bf16[4160,128]{1,0:T(8,128)(2,1)S(1)}, bf16[4160,128]{1,0:T(8,128)(2,1)S(1)}, u32[]{:S(2)}, u32[]{:S(2)}) collective-permute-start(bf16[4160,128]{1,0:T(8,128)(2,1)S(1)} %pad_maximum_fusion.1.refs_0_), channel_id=1, source_target_pairs={{0,4},{1,5},{2,6},{3,7},{4,0},{5,1},{6,2},{7,3},{8,12},{9,13},{10,... | collective-permute-start | bytes 3194888 | tf_op jit(solution)/shard_map/ppermute | solution.py:215
  48.4 2.2 %collective-permute-done.4 = bf16[2080,128]{1,0:T(8,128)(2,1)S(1)} collective-permute-done((bf16[2080,128]{1,0:T(8,128)(2,1)S(1)}, bf16[2080,128]{1,0:T(8,128)(2,1)S(1)}, u32[]{:S(2)}, u32[]{:S(2)}) %collective-permute-start.4) | collective-permute-done | bytes 532512 | tf_op jit(solution)/shard_map/ppermute | solution.py:215
  50.6 0.1 pad_maximum_fusion.refs_0_
  50.7 0.0 collective-permute-done.13.refs_1_
  50.7 5.4 %attend.6 = (f32[2,4,512,128]{3,2,1,0:T(8,128)S(1)}, f32[2,4,512,128]{3,2,1,0:T(8,128)S(1)}, f32[2,4,512,128]{3,2,1,0:T(8,128)S(1)}) custom-call(s32[2]{0:T(128)S(1)} %and_select_fusion.1.own_ids, bf16[2,4,512,128]{3,2,1,0:T(8,128)(2,1)S(1)} %bitcast.13, ...), custom_call_target="tpu_custom_call", output_to_operand_aliasing={{0}: (4, {}), {1}: (5, {}), {2}: (6, {})} | custom-call | flops 1073741824 | bytes 8388608 | tf_op jit(solution)/shard_map/attend/pallas_call | solution.py:167
  56.1 0.4 collective-permute-start.14
  56.5 2.4 %collective-permute-done.14.refs_1_ = bf16[4160,128]{1,0:T(8,128)(2,1)S(1)} collective-permute-done((bf16[4160,128]{1,0:T(8,128)(2,1)S(1)}, bf16[4160,128]{1,0:T(8,128)(2,1)S(1)}, u32[]{:S(2)}, u32[]{:S(2)}) %collective-permute-start.14) | collective-permute-done | bytes 1064992 | tf_op jit(solution)/shard_map/ppermute | solution.py:215
  58.8 9.1 %attend.7 = (bf16[128,32,128]{2,1,0:T(8,128)(2,1)}, f32[2,4,512,128]{3,2,1,0:T(8,128)S(1)}, f32[2,4,512,128]{3,2,1,0:T(8,128)S(1)}, f32[2,4,512,128]{3,2,1,0:T(8,128)S(1)}) custom-call(s32[2]{0:T(128)S(1)} %and_select_fusion.1.own_ids, bf16[2,4,512,128]{3,2,1,0:T(8,128)(2,1)S(1)} %bitcast.14, ...), custom_call_target="tpu_custom_call", output_to_operand_aliasing={{1}: (4, {}), {2}: (5, {}), {3}: (6, {})} | custom-call | flops 1073741824 | bytes 8388608 | tf_op jit(solution)/shard_map/attend/pallas_call | solution.py:167
  (8 shorter events, 0.2 us)
Async XLA Ops:
  1.9 13.0 %copy-start.1 = (s32[128]{0:T(128)S(1)}, s32[128]{0:T(128)}, u32[]{:S(2)}) copy-start(s32[128]{0:T(128)} %param.7) | copy-start | bytes 1540
  2.6 12.4 %copy-start = (bf16[128,32,128]{2,1,0:T(8,128)(2,1)S(1)}, bf16[128,32,128]{2,1,0:T(8,128)(2,1)}, u32[]{:S(2)}) copy-start(bf16[128,32,128]{2,1,0:T(8,128)(2,1)} %param.4) | copy-start | bytes 3145732
  2.7 9.1 %collective-permute-start = (bf16[1040,128]{1,0:T(8,128)(2,1)S(1)}, bf16[1040,128]{1,0:T(8,128)(2,1)S(1)}, u32[]{:S(2)}, u32[]{:S(2)}) collective-permute-start(bf16[1040,128]{1,0:T(8,128)(2,1)S(1)} %pad_maximum_fusion.8), channel_id=1, source_target_pairs={{0,8},{1,9},{2,10},{3,11},{4,12},{5,13},{6,14},{7,15},{8,24},{9,25... | collective-permute-start | bytes 798728 | tf_op jit(solution)/shard_map/ppermute | solution.py:215
  3.2 10.1 %collective-permute-start.9 = (bf16[1040,128]{1,0:T(8,128)(2,1)S(1)}, bf16[1040,128]{1,0:T(8,128)(2,1)S(1)}, u32[]{:S(2)}, u32[]{:S(2)}) collective-permute-start(bf16[1040,128]{1,0:T(8,128)(2,1)S(1)} %pad_maximum_fusion.8), channel_id=1, source_target_pairs={{0,1},{1,0},{2,3},{3,2},{4,6},{5,7},{6,4},{7,5},{8,9},{9,8},{10,11... | collective-permute-start | bytes 798728 | tf_op jit(solution)/shard_map/ppermute | solution.py:215
  11.8 9.2 %collective-permute-start.7 = (bf16[1040,128]{1,0:T(8,128)(2,1)S(1)}, bf16[1040,128]{1,0:T(8,128)(2,1)S(1)}, u32[]{:S(2)}, u32[]{:S(2)}) collective-permute-start(bf16[1040,128]{1,0:T(8,128)(2,1)S(1)} %collective-permute-done), channel_id=1, source_target_pairs={{0,1},{1,0},{2,3},{3,2},{4,6},{5,7},{6,4},{7,5},{8,9},{9,8},{10,11... | collective-permute-start | bytes 798728 | tf_op jit(solution)/shard_map/ppermute | solution.py:215
  13.3 10.9 %collective-permute-start.10 = (bf16[2080,128]{1,0:T(8,128)(2,1)S(1)}, bf16[2080,128]{1,0:T(8,128)(2,1)S(1)}, u32[]{:S(2)}, u32[]{:S(2)}) collective-permute-start(bf16[2080,128]{1,0:T(8,128)(2,1)S(1)} %pad_maximum_fusion.7), channel_id=1, source_target_pairs={{0,2},{1,3},{2,0},{3,1},{4,5},{5,4},{6,7},{7,6},{8,10},{9,11},{10,... | collective-permute-start | bytes 1597448 | tf_op jit(solution)/shard_map/ppermute | solution.py:215
  15.2 7.7 %collective-permute-start.1 = (bf16[1040,128]{1,0:T(8,128)(2,1)S(1)}, bf16[1040,128]{1,0:T(8,128)(2,1)S(1)}, u32[]{:S(2)}, u32[]{:S(2)}) collective-permute-start(bf16[1040,128]{1,0:T(8,128)(2,1)S(1)} %collective-permute-done), channel_id=1, source_target_pairs={{0,8},{1,9},{2,10},{3,11},{4,12},{5,13},{6,14},{7,15},{8,24},{9,25... | collective-permute-start | bytes 798728 | tf_op jit(solution)/shard_map/ppermute | solution.py:215
  21.0 13.7 %collective-permute-start.8 = (bf16[2080,128]{1,0:T(8,128)(2,1)S(1)}, bf16[2080,128]{1,0:T(8,128)(2,1)S(1)}, u32[]{:S(2)}, u32[]{:S(2)}) collective-permute-start(bf16[2080,128]{1,0:T(8,128)(2,1)S(1)} %pad_maximum_fusion.6), channel_id=1, source_target_pairs={{0,2},{1,3},{2,0},{3,1},{4,5},{5,4},{6,7},{7,6},{8,10},{9,11},{10,... | collective-permute-start | bytes 1597448 | tf_op jit(solution)/shard_map/ppermute | solution.py:215
  22.8 9.3 %collective-permute-start.5 = (bf16[1040,128]{1,0:T(8,128)(2,1)S(1)}, bf16[1040,128]{1,0:T(8,128)(2,1)S(1)}, u32[]{:S(2)}, u32[]{:S(2)}) collective-permute-start(bf16[1040,128]{1,0:T(8,128)(2,1)S(1)} %collective-permute-done.1), channel_id=1, source_target_pairs={{0,1},{1,0},{2,3},{3,2},{4,6},{5,7},{6,4},{7,5},{8,9},{9,8},{10,11... | collective-permute-start | bytes 798728 | tf_op jit(solution)/shard_map/ppermute | solution.py:215
  24.3 10.5 %collective-permute-start.11 = (bf16[4160,128]{1,0:T(8,128)(2,1)S(1)}, bf16[4160,128]{1,0:T(8,128)(2,1)S(1)}, u32[]{:S(2)}, u32[]{:S(2)}) collective-permute-start(bf16[4160,128]{1,0:T(8,128)(2,1)S(1)} %pad_maximum_fusion.3.refs_0_), channel_id=1, source_target_pairs={{0,4},{1,5},{2,6},{3,7},{4,0},{5,1},{6,2},{7,3},{8,12},{9,13},{10,... | collective-permute-start | bytes 3194888 | tf_op jit(solution)/shard_map/ppermute | solution.py:215
  24.4 9.7 %collective-permute-start.2 = (bf16[1040,128]{1,0:T(8,128)(2,1)S(1)}, bf16[1040,128]{1,0:T(8,128)(2,1)S(1)}, u32[]{:S(2)}, u32[]{:S(2)}) collective-permute-start(bf16[1040,128]{1,0:T(8,128)(2,1)S(1)} %collective-permute-done.1), channel_id=1, source_target_pairs={{0,8},{1,9},{2,10},{3,11},{4,12},{5,13},{6,14},{7,15},{8,24},{9,25... | collective-permute-start | bytes 798728 | tf_op jit(solution)/shard_map/ppermute | solution.py:215
  32.2 12.2 %collective-permute-start.6 = (bf16[2080,128]{1,0:T(8,128)(2,1)S(1)}, bf16[2080,128]{1,0:T(8,128)(2,1)S(1)}, u32[]{:S(2)}, u32[]{:S(2)}) collective-permute-start(bf16[2080,128]{1,0:T(8,128)(2,1)S(1)} %pad_maximum_fusion.5), channel_id=1, source_target_pairs={{0,2},{1,3},{2,0},{3,1},{4,5},{5,4},{6,7},{7,6},{8,10},{9,11},{10,... | collective-permute-start | bytes 1597448 | tf_op jit(solution)/shard_map/ppermute | solution.py:215
  34.1 7.1 %collective-permute-start.3 = (bf16[1040,128]{1,0:T(8,128)(2,1)S(1)}, bf16[1040,128]{1,0:T(8,128)(2,1)S(1)}, u32[]{:S(2)}, u32[]{:S(2)}) collective-permute-start(bf16[1040,128]{1,0:T(8,128)(2,1)S(1)} %collective-permute-done.2), channel_id=1, source_target_pairs={{0,1},{1,0},{2,3},{3,2},{4,6},{5,7},{6,4},{7,5},{8,9},{9,8},{10,11... | collective-permute-start | bytes 798728 | tf_op jit(solution)/shard_map/ppermute | solution.py:215
  41.1 3.3 %collective-permute-start.12 = (bf16[4160,128]{1,0:T(8,128)(2,1)S(1)}, bf16[4160,128]{1,0:T(8,128)(2,1)S(1)}, u32[]{:S(2)}, u32[]{:S(2)}) collective-permute-start(bf16[4160,128]{1,0:T(8,128)(2,1)S(1)} %pad_maximum_fusion.2.refs_0_), channel_id=1, source_target_pairs={{0,4},{1,5},{2,6},{3,7},{4,0},{5,1},{6,2},{7,3},{8,12},{9,13},{10,... | collective-permute-start | bytes 3194888 | tf_op jit(solution)/shard_map/ppermute | solution.py:215
  41.3 9.3 %collective-permute-start.4 = (bf16[2080,128]{1,0:T(8,128)(2,1)S(1)}, bf16[2080,128]{1,0:T(8,128)(2,1)S(1)}, u32[]{:S(2)}, u32[]{:S(2)}) collective-permute-start(bf16[2080,128]{1,0:T(8,128)(2,1)S(1)} %pad_maximum_fusion.4), channel_id=1, source_target_pairs={{0,2},{1,3},{2,0},{3,1},{4,5},{5,4},{6,7},{7,6},{8,10},{9,11},{10,... | collective-permute-start | bytes 1597448 | tf_op jit(solution)/shard_map/ppermute | solution.py:215
  47.6 3.0 %collective-permute-start.13 = (bf16[4160,128]{1,0:T(8,128)(2,1)S(1)}, bf16[4160,128]{1,0:T(8,128)(2,1)S(1)}, u32[]{:S(2)}, u32[]{:S(2)}) collective-permute-start(bf16[4160,128]{1,0:T(8,128)(2,1)S(1)} %pad_maximum_fusion.1.refs_0_), channel_id=1, source_target_pairs={{0,4},{1,5},{2,6},{3,7},{4,0},{5,1},{6,2},{7,3},{8,12},{9,13},{10,... | collective-permute-start | bytes 3194888 | tf_op jit(solution)/shard_map/ppermute | solution.py:215
  56.1 2.7 %collective-permute-start.14 = (bf16[4160,128]{1,0:T(8,128)(2,1)S(1)}, bf16[4160,128]{1,0:T(8,128)(2,1)S(1)}, u32[]{:S(2)}, u32[]{:S(2)}) collective-permute-start(bf16[4160,128]{1,0:T(8,128)(2,1)S(1)} %pad_maximum_fusion.refs_0_), channel_id=1, source_target_pairs={{0,4},{1,5},{2,6},{3,7},{4,0},{5,1},{6,2},{7,3},{8,12},{9,13},{10,... | collective-permute-start | bytes 3194888 | tf_op jit(solution)/shard_map/ppermute | solution.py:215

commit v3 on v2

--- a/solution.py
+++ b/solution.py
@@ -13,31 +13,32 @@
 AXES = ("outer", "inner")
 
 
-def flash(q, k, v, state, mask, factor):
+def scores(q, k):
+    score = lax.dot_general(
+        k, q, (((1,), (1,)), ((), ())), preferred_element_type=jnp.float32
+    )
+    return score.reshape(-1, 8, score.shape[1])
+
+
+def flash(score, v, state, factor):
     top, total, mixed = state
-    score = lax.dot_general(
-        q, k, (((1,), (1,)), ((), ())), preferred_element_type=jnp.float32
-    )
-    score = mask(score)
-    parts = [score[:, c : c + 128] for c in range(0, score.shape[1], 128)]
-    new = functools.reduce(jnp.maximum, parts)
-    new = jnp.max(new, axis=1, keepdims=True)
-    if top is None:
-        new = jnp.broadcast_to(new, parts[0].shape)
-    else:
+    new = jnp.max(jnp.max(score, axis=0), axis=0, keepdims=True)
+    new = jnp.broadcast_to(new, score.shape[1:])
+    if top is not None:
         new = jnp.maximum(top, new)
-    weights = [jnp.exp2((part - new) * factor) for part in parts]
-    part_total = functools.reduce(jnp.add, weights)
+    weight = jnp.exp2((score - new[None]) * factor)
+    part_total = jnp.sum(weight, axis=0)
     part_mixed = lax.dot_general(
-        jnp.concatenate([w.astype(jnp.bfloat16) for w in weights], axis=1),
-        v,
+        v.T,
+        weight.reshape(-1, weight.shape[2]).astype(jnp.bfloat16),
         (((1,), (0,)), ((), ())),
         preferred_element_type=jnp.float32,
     )
     if top is None:
         return new, part_total, part_mixed
     decay = jnp.exp2((top - new) * factor)
-    return new, total * decay + part_total, mixed * decay + part_mixed
+    mixed = mixed.reshape(-1, 8, mixed.shape[1]) * decay[None]
+    return new, total * decay + part_total, mixed.reshape(part_mixed.shape) + part_mixed
 
 
 def attend_kernel(group, factor, half, first, last, blocks, own_ids, q_ref, *refs):
@@ -52,36 +53,42 @@
         out_ref, refs = refs[0], refs[1:]
     top_ref, total_ref, mixed_ref, buf = refs
 
+    def tile(a, keys, values, mask=None, fresh=False):
+        ahead = scores(q_ref[a, 0], keys(0))
+        for h in range(heads_kv):
+            score = ahead
+            if h + 1 < heads_kv:
+                ahead = scores(q_ref[a, h + 1], keys(h + 1))
+            if mask is not None:
+                score = jnp.where(mask.reshape(score.shape), score, -jnp.inf)
+            state = (None, None, None)
+            if not fresh:
+                state = (top_ref[a, h], total_ref[a, h], mixed_ref[a, h])
+            state = flash(score, values(h), state, factor)
+            top_ref[a, h], total_ref[a, h], mixed_ref[a, h] = state
+
     if first:
         own_ref = kv_refs[0]
-        row_at = lax.broadcasted_iota(jnp.int32, (rows, 2 * RUN), 0) // group
-        col_at = lax.broadcasted_iota(jnp.int32, (rows, 2 * RUN), 1)
+
+        def own(g):
+            return jnp.concatenate(
+                [
+                    own_ref[r * run_rows + g * RUN : r * run_rows + (g + 1) * RUN]
+                    for r in range(2)
+                ]
+            )
+
+        key_at = lax.broadcasted_iota(jnp.int32, (2 * RUN, rows), 0)
+        row_at = lax.broadcasted_iota(jnp.int32, (2 * RUN, rows), 1) // group
         for a in range(2):
             mine, other = own_ids[a], own_ids[1 - a]
             seen = (other < mine) & ((other >= half) == (mine >= half))
             reach = jnp.where(seen, RUN, 0)
             if a == 0:
-                live = (col_at <= row_at) | ((col_at >= RUN) & (col_at < RUN + reach))
+                live = (key_at <= row_at) | ((key_at >= RUN) & (key_at < RUN + reach))
             else:
-                live = (col_at < reach) | ((col_at >= RUN) & (col_at - RUN <= row_at))
-            for h in range(heads_kv):
-                k, v = (
-                    jnp.concatenate(
-                        [
-                            own_ref[r * run_rows + g * RUN : r * run_rows + (g + 1) * RUN]
-                            for r in range(2)
-                        ]
-                    )
-                    for g in (h, heads_kv + h)
-                )
-                top_ref[a, h], total_ref[a, h], mixed_ref[a, h] = flash(
-                    q_ref[a, h],
-                    k,
-                    v,
-                    (None, None, None),
-                    lambda score: jnp.where(live, score, -jnp.inf),
-                    factor,
-                )
+                live = (key_at < reach) | ((key_at >= RUN) & (key_at - RUN <= row_at))
+            tile(a, own, lambda h: own(heads_kv + h), live, True)
 
     every = [
         (ref, n * block_rows)
@@ -106,7 +113,6 @@
             bits = jnp.sum(jnp.where(seen, bit, 0.0)).astype(jnp.int32)
             flags[a] += [(bits >> n) & 1 for n in range(2 * len(some))]
 
-    col = lax.broadcasted_iota(jnp.int32, (8, TILE * RUN), 1)
     for a in range(2):
         count = jnp.int32(0)
         for n in range(2 * len(every)):
@@ -118,34 +124,34 @@
                 buf[a, count] = ref[at : at + run_rows]
 
             count = count + flags[a][n]
-        for s in range(TILE - 1):
-            buf[a, count + s] = jnp.zeros(buf.shape[2:], buf.dtype)
+
+        def some_runs(start, runs):
+            def rows_of(g):
+                found = buf[a, pl.ds(start, runs), g * RUN : (g + 1) * RUN, :]
+                return found.reshape(runs * RUN, -1)
+
+            tile(a, rows_of, lambda h: rows_of(heads_kv + h))
 
         def step(item, carry):
-            bias = jnp.where(col < (count - item * TILE) * RUN, 0.0, -jnp.inf)[:1]
-            runs = pl.ds(item * TILE, TILE)
-            for h in range(heads_kv):
-                k = buf[a, runs, h * RUN : (h + 1) * RUN, :]
-                v = buf[a, runs, (heads_kv + h) * RUN : (heads_kv + h + 1) * RUN, :]
-                top_ref[a, h], total_ref[a, h], mixed_ref[a, h] = flash(
-                    q_ref[a, h],
-                    k.reshape(TILE * RUN, -1),
-                    v.reshape(TILE * RUN, -1),
-                    (top_ref[a, h], total_ref[a, h], mixed_ref[a, h]),
-                    lambda score: score + bias,
-                    factor,
-                )
+            some_runs(item * TILE, TILE)
             return carry
 
-        lax.fori_loop(0, (count + TILE - 1) // TILE, step, 0)
+        whole = count // TILE
+        lax.fori_loop(0, whole, step, 0)
+        for rest in range(1, TILE):
+
+            @pl.when(count - whole * TILE == rest)
+            def _():
+                some_runs(whole * TILE, rest)
 
     if last:
         for a in range(2):
             for h in range(0, heads_kv, 2):
                 done = []
                 for g in (h, h + 1):
-                    total = jnp.sum(total_ref[a, g], axis=1, keepdims=True)
-                    done.append((mixed_ref[a, g] / total).reshape(RUN, group, -1))
+                    total = jnp.sum(total_ref[a, g], axis=0, keepdims=True)
+                    part = mixed_ref[a, g] * (1.0 / total)
+                    done.append(part.T.reshape(RUN, group, -1))
                 out_ref[a * RUN : (a + 1) * RUN, h * group : (h + 2) * group, :] = (
                     jnp.concatenate(done, axis=1).astype(out_ref.dtype)
                 )
@@ -153,12 +159,15 @@
 
 def attend(own_ids, q, kvs, state, out, group, half, factor):
     first, last = state is None, out is not None
-    run_rows = 2 * q.shape[1] * RUN
+    heads_kv, rows, head_dim = q.shape[1:]
+    run_rows = 2 * heads_kv * RUN
     blocks = [x.shape[0] // (2 * run_rows + 16) for x in kvs]
     count = sum(blocks) - int(first)
     operands = [q, *kvs] + ([] if first else list(state))
-    lanes = jax.ShapeDtypeStruct(q.shape[:3] + (128,), jnp.float32)
-    carried = [lanes, lanes, jax.ShapeDtypeStruct(q.shape, jnp.float32)]
+    carried = [
+        jax.ShapeDtypeStruct((2, heads_kv, n, rows), jnp.float32)
+        for n in (8, 8, head_dim)
+    ]
     vmem = pl.BlockSpec(memory_space=pltpu.VMEM)
     shapes = ([out] if last else []) + carried
     aliases = {}
@@ -172,9 +181,7 @@
             grid=(),
             in_specs=[vmem] * len(operands),
             out_specs=[vmem] * len(shapes),
-            scratch_shapes=[
-                pltpu.VMEM((2, 2 * count + TILE - 1, run_rows, q.shape[3]), q.dtype)
-            ],
+            scratch_shapes=[pltpu.VMEM((2, 2 * count, run_rows, head_dim), q.dtype)],
         ),
         input_output_aliases=aliases,
         compiler_params=pltpu.CompilerParams(vmem_limit_bytes=24 * 1024 * 1024),

time: 67.5 us -> 66.6 us (0.987)
  the two profiles are of different devices: /device:TPU:24 before, /device:TPU:4 now
where the time goes in v3:
time: 66.6 us; the launch traced here: 66.9 us
  waiting for transfers between devices  27.3 us (41%)
  Pallas kernels  24.1 us (36%)
  starting transfers between devices  12 us (18%)
  local copies, waits for them, and re-layouts  2.14 us (3%)
  other arithmetic  1.21 us (2%)
    ppermute x15, waiting for transfers between devices, permute(): return lax.ppermute(x, AXES, pairs)  27.3 us
    pallas_call x4, Pallas kernels, attend(): pl.pallas_call(functools.partial(attend_kernel, group, factor, half, firs...  24.1 us
    ppermute x15, starting transfers between devices, permute(): return lax.ppermute(x, AXES, pairs)  12 us
    reshape x2, local copies, waits for them, and re-layouts, per_device(): x.reshape(2, RUN, heads_kv, head_dim)  1.85 us
  transfers between devices with their start and end apart: 15, of which 10 were waited for; matrix products, arithmetic and copies ran while one was open for 1% of the time, Pallas kernels for 17%

profile of v3, /device:TPU:4, one launch (start us, length us, event | category | flops | bytes accessed | tf_op | source)
XLA Modules:
  0.0 66.9 jit_solution(13811942031681568147)
XLA Ops:
  0.0 0.9 %copy.15 = bf16[2,64,4,128]{3,1,2,0:T(8,128)(2,1)S(1)} copy(bf16[2,64,4,128]{3,2,1,0:T(4,128)(2,1)} %bitcast.19) | data formatting | bytes 262144 | tf_op jit(solution)/shard_map/reshape | solution.py:242
  0.9 0.9 %copy.16 = bf16[2,64,4,128]{3,1,2,0:T(8,128)(2,1)S(1)} copy(bf16[2,64,4,128]{3,2,1,0:T(4,128)(2,1)} %bitcast.20) | data formatting | bytes 262144 | tf_op jit(solution)/shard_map/reshape | solution.py:242
  1.9 0.0 copy-start.1
  1.9 0.7 %fusion = bf16[128]{0:T(256)(128)(2,1)S(1)} fusion(s32[128]{0:T(128)} %param.7), kind=kLoop, calls=%fused_computation.19 | loop fusion | flops 2048 | bytes 768 | tf_op jit(solution)/shard_map/convert_element_type | solution.py:244
  2.6 0.0 copy-start
  2.7 1.6 %collective-permute-start = (bf16[1040,128]{1,0:T(8,128)(2,1)S(1)}, bf16[1040,128]{1,0:T(8,128)(2,1)S(1)}, u32[]{:S(2)}, u32[]{:S(2)}) collective-permute-start(bf16[1040,128]{1,0:T(8,128)(2,1)S(1)} %pad_maximum_fusion.8), channel_id=1, source_target_pairs={{0,8},{1,9},{2,10},{3,11},{4,12},{5,13},{6,14},{7,15},{8,24},{9,25... | collective-permute-start | bytes 798728 | tf_op jit(solution)/shard_map/ppermute | solution.py:222
  4.3 1.5 %collective-permute-start.9 = (bf16[1040,128]{1,0:T(8,128)(2,1)S(1)}, bf16[1040,128]{1,0:T(8,128)(2,1)S(1)}, u32[]{:S(2)}, u32[]{:S(2)}) collective-permute-start(bf16[1040,128]{1,0:T(8,128)(2,1)S(1)} %pad_maximum_fusion.8), channel_id=1, source_target_pairs={{0,1},{1,0},{2,3},{3,2},{4,6},{5,7},{6,4},{7,5},{8,9},{9,8},{10,11... | collective-permute-start | bytes 798728 | tf_op jit(solution)/shard_map/ppermute | solution.py:222
  5.8 6.0 %collective-permute-done = bf16[1040,128]{1,0:T(8,128)(2,1)S(1)} collective-permute-done((bf16[1040,128]{1,0:T(8,128)(2,1)S(1)}, bf16[1040,128]{1,0:T(8,128)(2,1)S(1)}, u32[]{:S(2)}, u32[]{:S(2)}) %collective-permute-start) | collective-permute-done | bytes 266272 | tf_op jit(solution)/shard_map/ppermute | solution.py:222
  11.8 1.5 %collective-permute-start.7 = (bf16[1040,128]{1,0:T(8,128)(2,1)S(1)}, bf16[1040,128]{1,0:T(8,128)(2,1)S(1)}, u32[]{:S(2)}, u32[]{:S(2)}) collective-permute-start(bf16[1040,128]{1,0:T(8,128)(2,1)S(1)} %collective-permute-done), channel_id=1, source_target_pairs={{0,1},{1,0},{2,3},{3,2},{4,6},{5,7},{6,4},{7,5},{8,9},{9,8},{10,11... | collective-permute-start | bytes 798728 | tf_op jit(solution)/shard_map/ppermute | solution.py:222
  13.3 0.0 collective-permute-done.9
  13.3 0.6 collective-permute-start.10
  13.9 0.0 copy-done.1
  13.9 0.1 slice.3
  14.0 0.0 copy-done
  14.0 0.2 copy.18
  14.1 0.8 %collective-permute-start.1 = (bf16[1040,128]{1,0:T(8,128)(2,1)S(1)}, bf16[1040,128]{1,0:T(8,128)(2,1)S(1)}, u32[]{:S(2)}, u32[]{:S(2)}) collective-permute-start(bf16[1040,128]{1,0:T(8,128)(2,1)S(1)} %collective-permute-done), channel_id=1, source_target_pairs={{0,8},{1,9},{2,10},{3,11},{4,12},{5,13},{6,14},{7,15},{8,24},{9,25... | collective-permute-start | bytes 798728 | tf_op jit(solution)/shard_map/ppermute | solution.py:222
  15.0 6.1 %collective-permute-done.7 = bf16[1040,128]{1,0:T(8,128)(2,1)S(1)} collective-permute-done((bf16[1040,128]{1,0:T(8,128)(2,1)S(1)}, bf16[1040,128]{1,0:T(8,128)(2,1)S(1)}, u32[]{:S(2)}, u32[]{:S(2)}) %collective-permute-start.7) | collective-permute-done | bytes 266272 | tf_op jit(solution)/shard_map/ppermute | solution.py:222
  21.1 0.4 collective-permute-start.8
  21.5 0.3 collective-permute-done.1
  21.8 1.3 %collective-permute-start.5 = (bf16[1040,128]{1,0:T(8,128)(2,1)S(1)}, bf16[1040,128]{1,0:T(8,128)(2,1)S(1)}, u32[]{:S(2)}, u32[]{:S(2)}) collective-permute-start(bf16[1040,128]{1,0:T(8,128)(2,1)S(1)} %collective-permute-done.1), channel_id=1, source_target_pairs={{0,1},{1,0},{2,3},{3,2},{4,6},{5,7},{6,4},{7,5},{8,9},{9,8},{10,11... | collective-permute-start | bytes 798728 | tf_op jit(solution)/shard_map/ppermute | solution.py:222
  23.1 0.2 collective-permute-done.10
  23.3 0.1 pad_maximum_fusion.3.refs_0_
  23.4 0.1 collective-permute-start.11
  23.5 0.8 %collective-permute-start.2 = (bf16[1040,128]{1,0:T(8,128)(2,1)S(1)}, bf16[1040,128]{1,0:T(8,128)(2,1)S(1)}, u32[]{:S(2)}, u32[]{:S(2)}) collective-permute-start(bf16[1040,128]{1,0:T(8,128)(2,1)S(1)} %collective-permute-done.1), channel_id=1, source_target_pairs={{0,8},{1,9},{2,10},{3,11},{4,12},{5,13},{6,14},{7,15},{8,24},{9,25... | collective-permute-start | bytes 798728 | tf_op jit(solution)/shard_map/ppermute | solution.py:222
  24.3 6.8 %collective-permute-done.5 = bf16[1040,128]{1,0:T(8,128)(2,1)S(1)} collective-permute-done((bf16[1040,128]{1,0:T(8,128)(2,1)S(1)}, bf16[1040,128]{1,0:T(8,128)(2,1)S(1)}, u32[]{:S(2)}, u32[]{:S(2)}) %collective-permute-start.5) | collective-permute-done | bytes 266272 | tf_op jit(solution)/shard_map/ppermute | solution.py:222
  31.2 1.6 %collective-permute-start.6 = (bf16[2080,128]{1,0:T(8,128)(2,1)S(1)}, bf16[2080,128]{1,0:T(8,128)(2,1)S(1)}, u32[]{:S(2)}, u32[]{:S(2)}) collective-permute-start(bf16[2080,128]{1,0:T(8,128)(2,1)S(1)} %pad_maximum_fusion.5), channel_id=1, source_target_pairs={{0,2},{1,3},{2,0},{3,1},{4,5},{5,4},{6,7},{7,6},{8,10},{9,11},{10,... | collective-permute-start | bytes 1597448 | tf_op jit(solution)/shard_map/ppermute | solution.py:222
  32.8 0.5 collective-permute-done.2
  33.2 0.9 %collective-permute-start.3 = (bf16[1040,128]{1,0:T(8,128)(2,1)S(1)}, bf16[1040,128]{1,0:T(8,128)(2,1)S(1)}, u32[]{:S(2)}, u32[]{:S(2)}) collective-permute-start(bf16[1040,128]{1,0:T(8,128)(2,1)S(1)} %collective-permute-done.2), channel_id=1, source_target_pairs={{0,1},{1,0},{2,3},{3,2},{4,6},{5,7},{6,4},{7,5},{8,9},{9,8},{10,11... | collective-permute-start | bytes 798728 | tf_op jit(solution)/shard_map/ppermute | solution.py:222
  34.2 0.0 collective-permute-done.8
  34.2 0.1 pad_maximum_fusion.2.refs_0_
  34.2 0.0 collective-permute-done.11.refs_1_
  34.2 6.2 %attend.4 = (f32[2,4,8,512]{3,2,1,0:T(8,128)S(1)}, f32[2,4,8,512]{3,2,1,0:T(8,128)S(1)}, f32[2,4,128,512]{3,2,1,0:T(8,128)S(1)}) custom-call(s32[2]{0:T(128)S(1)} %and_select_fusion.1.own_ids, bf16[2,4,512,128]{3,2,1,0:T(8,128)(2,1)S(1)} %bitcast.11, bf16[4160,128]{1,0:T(8,128)(2,1)S(1)} %pad_maximum_fusion.3.refs_0_, ...), custom_call_target="tpu_custom_call" | custom-call | flops 939524096 | bytes 8388608 | tf_op jit(solution)/shard_map/attend/pallas_call | solution.py:176
  40.4 0.1 collective-permute-start.12
  40.5 0.0 collective-permute-done.3
  40.5 0.6 collective-permute-start.4
  41.1 2.2 %collective-permute-done.6 = bf16[2080,128]{1,0:T(8,128)(2,1)S(1)} collective-permute-done((bf16[2080,128]{1,0:T(8,128)(2,1)S(1)}, bf16[2080,128]{1,0:T(8,128)(2,1)S(1)}, u32[]{:S(2)}, u32[]{:S(2)}) %collective-permute-start.6) | collective-permute-done | bytes 532512 | tf_op jit(solution)/shard_map/ppermute | solution.py:222
  43.4 0.1 pad_maximum_fusion.1.refs_0_
  43.4 0.0 collective-permute-done.12.refs_1_
  43.4 5.5 %attend.5 = (f32[2,4,8,512]{3,2,1,0:T(8,128)S(1)}, f32[2,4,8,512]{3,2,1,0:T(8,128)S(1)}, f32[2,4,128,512]{3,2,1,0:T(8,128)S(1)}) custom-call(s32[2]{0:T(128)S(1)} %and_select_fusion.1.own_ids, bf16[2,4,512,128]{3,2,1,0:T(8,128)(2,1)S(1)} %bitcast.12, ...), custom_call_target="tpu_custom_call", output_to_operand_aliasing={{0}: (4, {}), {1}: (5, {}), {2}: (6, {})} | custom-call | flops 1073741824 | bytes 8388608 | tf_op jit(solution)/shard_map/attend/pallas_call | solution.py:176
  49.0 0.1 collective-permute-start.13
  49.1 0.8 %collective-permute-done.4 = bf16[2080,128]{1,0:T(8,128)(2,1)S(1)} collective-permute-done((bf16[2080,128]{1,0:T(8,128)(2,1)S(1)}, bf16[2080,128]{1,0:T(8,128)(2,1)S(1)}, u32[]{:S(2)}, u32[]{:S(2)}) %collective-permute-start.4) | collective-permute-done | bytes 532512 | tf_op jit(solution)/shard_map/ppermute | solution.py:222
  49.9 0.1 pad_maximum_fusion.refs_0_
  50.0 1.8 %collective-permute-done.13.refs_1_ = bf16[4160,128]{1,0:T(8,128)(2,1)S(1)} collective-permute-done((bf16[4160,128]{1,0:T(8,128)(2,1)S(1)}, bf16[4160,128]{1,0:T(8,128)(2,1)S(1)}, u32[]{:S(2)}, u32[]{:S(2)}) %collective-permute-start.13) | collective-permute-done | bytes 1064992 | tf_op jit(solution)/shard_map/ppermute | solution.py:222
  51.7 5.6 %attend.6 = (f32[2,4,8,512]{3,2,1,0:T(8,128)S(1)}, f32[2,4,8,512]{3,2,1,0:T(8,128)S(1)}, f32[2,4,128,512]{3,2,1,0:T(8,128)S(1)}) custom-call(s32[2]{0:T(128)S(1)} %and_select_fusion.1.own_ids, bf16[2,4,512,128]{3,2,1,0:T(8,128)(2,1)S(1)} %bitcast.13, ...), custom_call_target="tpu_custom_call", output_to_operand_aliasing={{0}: (4, {}), {1}: (5, {}), {2}: (6, {})} | custom-call | flops 1073741824 | bytes 8388608 | tf_op jit(solution)/shard_map/attend/pallas_call | solution.py:176
  57.3 0.1 collective-permute-start.14
  57.4 2.7 %collective-permute-done.14.refs_1_ = bf16[4160,128]{1,0:T(8,128)(2,1)S(1)} collective-permute-done((bf16[4160,128]{1,0:T(8,128)(2,1)S(1)}, bf16[4160,128]{1,0:T(8,128)(2,1)S(1)}, u32[]{:S(2)}, u32[]{:S(2)}) %collective-permute-start.14) | collective-permute-done | bytes 1064992 | tf_op jit(solution)/shard_map/ppermute | solution.py:222
  60.1 6.8 %attend.7 = (bf16[128,32,128]{2,1,0:T(8,128)(2,1)}, f32[2,4,8,512]{3,2,1,0:T(8,128)S(1)}, f32[2,4,8,512]{3,2,1,0:T(8,128)S(1)}, f32[2,4,128,512]{3,2,1,0:T(8,128)S(1)}) custom-call(s32[2]{0:T(128)S(1)} %and_select_fusion.1.own_ids, bf16[2,4,512,128]{3,2,1,0:T(8,128)(2,1)S(1)} %bitcast.14, ...), custom_call_target="tpu_custom_call", output_to_operand_aliasing={{1}: (4, {}), {2}: (5, {}), {3}: (6, {})} | custom-call | flops 1073741824 | bytes 8388608 | tf_op jit(solution)/shard_map/attend/pallas_call | solution.py:176
  (8 shorter events, 0.2 us)
Async XLA Ops:
  1.9 12.0 %copy-start.1 = (s32[128]{0:T(128)S(1)}, s32[128]{0:T(128)}, u32[]{:S(2)}) copy-start(s32[128]{0:T(128)} %param.7) | copy-start | bytes 1540
  2.6 11.4 %copy-start = (bf16[128,32,128]{2,1,0:T(8,128)(2,1)S(1)}, bf16[128,32,128]{2,1,0:T(8,128)(2,1)}, u32[]{:S(2)}) copy-start(bf16[128,32,128]{2,1,0:T(8,128)(2,1)} %param.4) | copy-start | bytes 3145732
  2.7 9.1 %collective-permute-start = (bf16[1040,128]{1,0:T(8,128)(2,1)S(1)}, bf16[1040,128]{1,0:T(8,128)(2,1)S(1)}, u32[]{:S(2)}, u32[]{:S(2)}) collective-permute-start(bf16[1040,128]{1,0:T(8,128)(2,1)S(1)} %pad_maximum_fusion.8), channel_id=1, source_target_pairs={{0,8},{1,9},{2,10},{3,11},{4,12},{5,13},{6,14},{7,15},{8,24},{9,25... | collective-permute-start | bytes 798728 | tf_op jit(solution)/shard_map/ppermute | solution.py:222
  4.3 9.0 %collective-permute-start.9 = (bf16[1040,128]{1,0:T(8,128)(2,1)S(1)}, bf16[1040,128]{1,0:T(8,128)(2,1)S(1)}, u32[]{:S(2)}, u32[]{:S(2)}) collective-permute-start(bf16[1040,128]{1,0:T(8,128)(2,1)S(1)} %pad_maximum_fusion.8), channel_id=1, source_target_pairs={{0,1},{1,0},{2,3},{3,2},{4,6},{5,7},{6,4},{7,5},{8,9},{9,8},{10,11... | collective-permute-start | bytes 798728 | tf_op jit(solution)/shard_map/ppermute | solution.py:222
  11.8 9.3 %collective-permute-start.7 = (bf16[1040,128]{1,0:T(8,128)(2,1)S(1)}, bf16[1040,128]{1,0:T(8,128)(2,1)S(1)}, u32[]{:S(2)}, u32[]{:S(2)}) collective-permute-start(bf16[1040,128]{1,0:T(8,128)(2,1)S(1)} %collective-permute-done), channel_id=1, source_target_pairs={{0,1},{1,0},{2,3},{3,2},{4,6},{5,7},{6,4},{7,5},{8,9},{9,8},{10,11... | collective-permute-start | bytes 798728 | tf_op jit(solution)/shard_map/ppermute | solution.py:222
  13.3 10.0 %collective-permute-start.10 = (bf16[2080,128]{1,0:T(8,128)(2,1)S(1)}, bf16[2080,128]{1,0:T(8,128)(2,1)S(1)}, u32[]{:S(2)}, u32[]{:S(2)}) collective-permute-start(bf16[2080,128]{1,0:T(8,128)(2,1)S(1)} %pad_maximum_fusion.7), channel_id=1, source_target_pairs={{0,2},{1,3},{2,0},{3,1},{4,5},{5,4},{6,7},{7,6},{8,10},{9,11},{10,... | collective-permute-start | bytes 1597448 | tf_op jit(solution)/shard_map/ppermute | solution.py:222
  14.1 7.7 %collective-permute-start.1 = (bf16[1040,128]{1,0:T(8,128)(2,1)S(1)}, bf16[1040,128]{1,0:T(8,128)(2,1)S(1)}, u32[]{:S(2)}, u32[]{:S(2)}) collective-permute-start(bf16[1040,128]{1,0:T(8,128)(2,1)S(1)} %collective-permute-done), channel_id=1, source_target_pairs={{0,8},{1,9},{2,10},{3,11},{4,12},{5,13},{6,14},{7,15},{8,24},{9,25... | collective-permute-start | bytes 798728 | tf_op jit(solution)/shard_map/ppermute | solution.py:222
  21.1 13.0 %collective-permute-start.8 = (bf16[2080,128]{1,0:T(8,128)(2,1)S(1)}, bf16[2080,128]{1,0:T(8,128)(2,1)S(1)}, u32[]{:S(2)}, u32[]{:S(2)}) collective-permute-start(bf16[2080,128]{1,0:T(8,128)(2,1)S(1)} %pad_maximum_fusion.6), channel_id=1, source_target_pairs={{0,2},{1,3},{2,0},{3,1},{4,5},{5,4},{6,7},{7,6},{8,10},{9,11},{10,... | collective-permute-start | bytes 1597448 | tf_op jit(solution)/shard_map/ppermute | solution.py:222
  21.8 9.3 %collective-permute-start.5 = (bf16[1040,128]{1,0:T(8,128)(2,1)S(1)}, bf16[1040,128]{1,0:T(8,128)(2,1)S(1)}, u32[]{:S(2)}, u32[]{:S(2)}) collective-permute-start(bf16[1040,128]{1,0:T(8,128)(2,1)S(1)} %collective-permute-done.1), channel_id=1, source_target_pairs={{0,1},{1,0},{2,3},{3,2},{4,6},{5,7},{6,4},{7,5},{8,9},{9,8},{10,11... | collective-permute-start | bytes 798728 | tf_op jit(solution)/shard_map/ppermute | solution.py:222
  23.4 10.9 %collective-permute-start.11 = (bf16[4160,128]{1,0:T(8,128)(2,1)S(1)}, bf16[4160,128]{1,0:T(8,128)(2,1)S(1)}, u32[]{:S(2)}, u32[]{:S(2)}) collective-permute-start(bf16[4160,128]{1,0:T(8,128)(2,1)S(1)} %pad_maximum_fusion.3.refs_0_), channel_id=1, source_target_pairs={{0,4},{1,5},{2,6},{3,7},{4,0},{5,1},{6,2},{7,3},{8,12},{9,13},{10,... | collective-permute-start | bytes 3194888 | tf_op jit(solution)/shard_map/ppermute | solution.py:222
  23.5 9.7 %collective-permute-start.2 = (bf16[1040,128]{1,0:T(8,128)(2,1)S(1)}, bf16[1040,128]{1,0:T(8,128)(2,1)S(1)}, u32[]{:S(2)}, u32[]{:S(2)}) collective-permute-start(bf16[1040,128]{1,0:T(8,128)(2,1)S(1)} %collective-permute-done.1), channel_id=1, source_target_pairs={{0,8},{1,9},{2,10},{3,11},{4,12},{5,13},{6,14},{7,15},{8,24},{9,25... | collective-permute-start | bytes 798728 | tf_op jit(solution)/shard_map/ppermute | solution.py:222
  31.2 12.2 %collective-permute-start.6 = (bf16[2080,128]{1,0:T(8,128)(2,1)S(1)}, bf16[2080,128]{1,0:T(8,128)(2,1)S(1)}, u32[]{:S(2)}, u32[]{:S(2)}) collective-permute-start(bf16[2080,128]{1,0:T(8,128)(2,1)S(1)} %pad_maximum_fusion.5), channel_id=1, source_target_pairs={{0,2},{1,3},{2,0},{3,1},{4,5},{5,4},{6,7},{7,6},{8,10},{9,11},{10,... | collective-permute-start | bytes 1597448 | tf_op jit(solution)/shard_map/ppermute | solution.py:222
  33.2 7.3 %collective-permute-start.3 = (bf16[1040,128]{1,0:T(8,128)(2,1)S(1)}, bf16[1040,128]{1,0:T(8,128)(2,1)S(1)}, u32[]{:S(2)}, u32[]{:S(2)}) collective-permute-start(bf16[1040,128]{1,0:T(8,128)(2,1)S(1)} %collective-permute-done.2), channel_id=1, source_target_pairs={{0,1},{1,0},{2,3},{3,2},{4,6},{5,7},{6,4},{7,5},{8,9},{9,8},{10,11... | collective-permute-start | bytes 798728 | tf_op jit(solution)/shard_map/ppermute | solution.py:222
  40.4 3.0 %collective-permute-start.12 = (bf16[4160,128]{1,0:T(8,128)(2,1)S(1)}, bf16[4160,128]{1,0:T(8,128)(2,1)S(1)}, u32[]{:S(2)}, u32[]{:S(2)}) collective-permute-start(bf16[4160,128]{1,0:T(8,128)(2,1)S(1)} %pad_maximum_fusion.2.refs_0_), channel_id=1, source_target_pairs={{0,4},{1,5},{2,6},{3,7},{4,0},{5,1},{6,2},{7,3},{8,12},{9,13},{10,... | collective-permute-start | bytes 3194888 | tf_op jit(solution)/shard_map/ppermute | solution.py:222
  40.5 9.3 %collective-permute-start.4 = (bf16[2080,128]{1,0:T(8,128)(2,1)S(1)}, bf16[2080,128]{1,0:T(8,128)(2,1)S(1)}, u32[]{:S(2)}, u32[]{:S(2)}) collective-permute-start(bf16[2080,128]{1,0:T(8,128)(2,1)S(1)} %pad_maximum_fusion.4), channel_id=1, source_target_pairs={{0,2},{1,3},{2,0},{3,1},{4,5},{5,4},{6,7},{7,6},{8,10},{9,11},{10,... | collective-permute-start | bytes 1597448 | tf_op jit(solution)/shard_map/ppermute | solution.py:222
  49.0 2.7 %collective-permute-start.13 = (bf16[4160,128]{1,0:T(8,128)(2,1)S(1)}, bf16[4160,128]{1,0:T(8,128)(2,1)S(1)}, u32[]{:S(2)}, u32[]{:S(2)}) collective-permute-start(bf16[4160,128]{1,0:T(8,128)(2,1)S(1)} %pad_maximum_fusion.1.refs_0_), channel_id=1, source_target_pairs={{0,4},{1,5},{2,6},{3,7},{4,0},{5,1},{6,2},{7,3},{8,12},{9,13},{10,... | collective-permute-start | bytes 3194888 | tf_op jit(solution)/shard_map/ppermute | solution.py:222
  57.3 2.7 %collective-permute-start.14 = (bf16[4160,128]{1,0:T(8,128)(2,1)S(1)}, bf16[4160,128]{1,0:T(8,128)(2,1)S(1)}, u32[]{:S(2)}, u32[]{:S(2)}) collective-permute-start(bf16[4160,128]{1,0:T(8,128)(2,1)S(1)} %pad_maximum_fusion.refs_0_), channel_id=1, source_target_pairs={{0,4},{1,5},{2,6},{3,7},{4,0},{5,1},{6,2},{7,3},{8,12},{9,13},{10,... | collective-permute-start | bytes 3194888 | tf_op jit(solution)/shard_map/ppermute | solution.py:222
